TPU v7x, 32 devices: a whole 2x2x4 slice. The times are simulated.
32 devices in a mesh: dp: 16 (over z, x, core), seq: 2 (over y).
Axes of the slice: x: 2, y: 2, z: 4, core: 2. Of those that a mesh axis runs over, the one named last changes fastest.
Arguments:
- block_entry_tokens: bfloat16 [16, 1024, 1024], P('dp', 'seq'), may hold values from -6 to 6
- result_cotangent: bfloat16 [16, 1024, 1024], P('dp', 'seq'), may hold values from -6 to 6
- leading_scale_factor: bfloat16 [1024], P('dp'), may hold values from 0.5 to 1.5
- leading_bias_vector: bfloat16 [1024], P('dp'), may hold values from -3 to 3
- query_key_value_matrix: bfloat16 [1024, 3072], P('dp'), may hold values from -0.25 to 0.25
- query_key_value_bias: bfloat16 [3072], P('dp'), may hold values from -3 to 3
- attention_exit_matrix: bfloat16 [1024, 1024], P('dp'), may hold values from -0.75 to 0.75
- attention_exit_bias: bfloat16 [1024], P('dp'), may hold values from -3 to 3
- latter_scale_factor: bfloat16 [1024], P('dp'), may hold values from 0.5 to 1.5
- latter_bias_vector: bfloat16 [1024], P('dp'), may hold values from -3 to 3
- expand_projection_matrix: bfloat16 [1024, 4096], P('dp'), may hold values from -0.1875 to 0.1875
- expand_projection_offset: bfloat16 [4096], P('dp'), may hold values from -3 to 3
- contract_projection_matrix: bfloat16 [4096, 1024], P('dp'), may hold values from -0.09375 to 0.09375
- contract_projection_offset: bfloat16 [1024], P('dp'), may hold values from -3 to 3
Outputs:
- block_output: float32 [16, 1024, 1024], P('dp', 'seq')
- input_grad: float32 [16, 1024, 1024], P('dp', 'seq')
- prenorm_gain_gradient: float32 [1024], P('dp')
- prenorm_shift_gradient: float32 [1024], P('dp')
- qkvmatrix_grad: float32 [1024, 3072], P('dp')
- qkvshift_grad: float32 [3072], P('dp')
- outmatrix_grad: float32 [1024, 1024], P('dp')
- outshift_grad: float32 [1024], P('dp')
- midgain_grad: float32 [1024], P('dp')
- midshift_grad: float32 [1024], P('dp')
- upmatrix_grad: float32 [1024, 4096], P('dp')
- upshift_grad: float32 [4096], P('dp')
- downmatrix_grad: float32 [4096, 1024], P('dp')
- downshift_grad: float32 [1024], P('dp')
All inputs are finite; a program needn't handle non-finite values.
Results may differ from a plain program's by a relative error of at most 0.019.
Values may be sent and summed in bfloat16 or wider, within the bound.
A program may use at most 192 MiB of HBM per device.

v0:
```python
import jax
import jax.numpy as jnp
from jax import lax
from jax.sharding import PartitionSpec as P

HD = 64


EPS = 1e-05
NEG = -1e30


def standardize_features(values, gain, shift):
    center = values - jnp.mean(values, -1, keepdims=True)
    spread = jnp.mean(center * center, -1, keepdims=True)
    return center * lax.rsqrt(spread + EPS) * gain + shift


def gelu_apply(values):
    return jax.nn.gelu(values, approximate=True)


def head_masks(local_width):
    column_head = lax.broadcasted_iota(jnp.int32, (1, local_width), 1) // HD
    return [(column_head == head).astype(jnp.bfloat16) for head in range(local_width // HD)]


def masked_scores(qmasked, keypart, offset, factor):
    scores = (
        lax.dot_general(
            qmasked, keypart, (((1,), (1,)), ((), ())), preferred_element_type=jnp.float32
        )
        * factor
    )
    query_pos = offset + lax.broadcasted_iota(jnp.int32, scores.shape, 0)
    key_pos = lax.broadcasted_iota(jnp.int32, scores.shape, 1)
    return jnp.where(key_pos <= query_pos, scores, NEG)


def attend(heads_in):
    length = heads_in.shape[0]
    local_width = heads_in.shape[2]
    span_rows = min(512, length)
    factor = HD ** (-0.5)
    queries, keyset, values = (heads_in[:, 0], heads_in[:, 1], heads_in[:, 2])
    masks = head_masks(local_width)
    contexts = []
    logsums = []
    for number in range(length // span_rows):
        offset = number * span_rows
        key_end = offset + span_rows
        qblock = queries[offset:key_end]
        keypart = keyset[:key_end]
        valuepart = values[:key_end]
        context = jnp.zeros((span_rows, local_width), jnp.float32)
        block_sums = []
        for mask in masks:
            scores = masked_scores(qblock * mask, keypart, offset, factor)
            highest = jnp.max(scores, -1, keepdims=True)
            powers = jnp.exp(scores - highest)
            totals = jnp.sum(powers, -1, keepdims=True)
            probab = (powers / totals).astype(jnp.bfloat16)
            context = context + jnp.dot(
                probab, valuepart * mask, preferred_element_type=jnp.float32
            )
            block_sums.append(highest + jnp.log(totals))
        contexts.append(context)
        logsums.append(block_sums)
    return (jnp.concatenate(contexts, 0), logsums)


def attend_back(heads_in, logsums, ctx_delta):
    length = heads_in.shape[0]
    local_width = heads_in.shape[2]
    span_rows = min(512, length)
    factor = HD ** (-0.5)
    queries, keyset, values = (heads_in[:, 0], heads_in[:, 1], heads_in[:, 2])
    masks = head_masks(local_width)
    key_acc = jnp.zeros((length, local_width), jnp.float32)
    value_acc = jnp.zeros((length, local_width), jnp.float32)
    query_parts = []
    for number in range(length // span_rows):
        offset = number * span_rows
        key_end = offset + span_rows
        qblock = queries[offset:key_end]
        gblock = ctx_delta[offset:key_end]
        keypart = keyset[:key_end]
        valuepart = values[:key_end]
        qdelta = jnp.zeros((span_rows, local_width), jnp.float32)
        key_part_acc = jnp.zeros((key_end, local_width), jnp.float32)
        value_part_acc = jnp.zeros((key_end, local_width), jnp.float32)
        for index, mask in enumerate(masks):
            qmasked = qblock * mask
            scores = masked_scores(qmasked, keypart, offset, factor)
            probab = jnp.exp(scores - logsums[number][index])
            pdelta = lax.dot_general(
                gblock,
                valuepart * mask,
                (((1,), (1,)), ((), ())),
                preferred_element_type=jnp.float32,
            )
            inner_sum = jnp.sum(probab * pdelta, -1, keepdims=True)
            sdelta = (probab * (pdelta - inner_sum)).astype(jnp.bfloat16)
            qdelta = (
                qdelta
                + jnp.dot(sdelta, keypart * mask, preferred_element_type=jnp.float32) * factor
            )
            key_part_acc = (
                key_part_acc
                + lax.dot_general(
                    sdelta, qmasked, (((0,), (0,)), ((), ())), preferred_element_type=jnp.float32
                )
                * factor
            )
            value_part_acc = value_part_acc + lax.dot_general(
                probab.astype(jnp.bfloat16),
                gblock * mask,
                (((0,), (0,)), ((), ())),
                preferred_element_type=jnp.float32,
            )
        key_acc = key_acc.at[:key_end].add(key_part_acc)
        value_acc = value_acc.at[:key_end].add(value_part_acc)
        query_parts.append(qdelta)
    stacked = jnp.stack([jnp.concatenate(query_parts, 0), key_acc, value_acc], 1)
    return stacked.astype(jnp.bfloat16)


def local(
    block_entry_tokens,
    result_cotangent,
    leading_scale_factor,
    leading_bias_vector,
    query_key_value_matrix,
    query_key_value_bias,
    attention_exit_matrix,
    attention_exit_bias,
    latter_scale_factor,
    latter_bias_vector,
    expand_projection_matrix,
    expand_projection_offset,
    contract_projection_matrix,
    contract_projection_offset,
):
    hidden = block_entry_tokens.reshape(-1, block_entry_tokens.shape[-1]).astype(jnp.float32)
    tokens = hidden.shape[0]
    width = hidden.shape[1]
    attn_whole = (
        lax.all_gather(leading_scale_factor, "dp", axis=0, tiled=True),
        lax.all_gather(leading_bias_vector, "dp", axis=0, tiled=True),
        lax.all_gather(query_key_value_matrix, "dp", axis=0, tiled=True),
        lax.all_gather(query_key_value_bias, "dp", axis=0, tiled=True),
        lax.all_gather(attention_exit_matrix, "dp", axis=0, tiled=True),
        lax.all_gather(attention_exit_bias, "dp", axis=0, tiled=True),
    )
    gain_one, shift_one, w_qkv, b_qkv, w_out, b_out = attn_whole
    normed_one, first_pullback_step = jax.vjp(
        standardize_features, hidden, gain_one.astype(jnp.float32), shift_one.astype(jnp.float32)
    )
    h_one = normed_one.astype(jnp.bfloat16)
    qkv_lin = jnp.dot(h_one, w_qkv, preferred_element_type=jnp.float32) + b_qkv.astype(jnp.float32)
    qkv_low = qkv_lin.astype(jnp.bfloat16).reshape(tokens, 3, width)
    heads_in = lax.all_to_all(qkv_low, "seq", split_axis=2, concat_axis=0, tiled=True)
    context, logsums = attend(heads_in)
    ctx_tok = lax.all_to_all(
        context.astype(jnp.bfloat16), "seq", split_axis=0, concat_axis=1, tiled=True
    )
    resid = (
        hidden
        + jnp.dot(ctx_tok, w_out, preferred_element_type=jnp.float32)
        + b_out.astype(jnp.float32)
    )
    mlp_whole = (
        lax.all_gather(latter_scale_factor, "dp", axis=0, tiled=True),
        lax.all_gather(latter_bias_vector, "dp", axis=0, tiled=True),
        lax.all_gather(expand_projection_matrix, "dp", axis=0, tiled=True),
        lax.all_gather(expand_projection_offset, "dp", axis=0, tiled=True),
        lax.all_gather(contract_projection_matrix, "dp", axis=0, tiled=True),
        lax.all_gather(contract_projection_offset, "dp", axis=0, tiled=True),
    )
    gain_two, shift_two, w_up, b_up, w_down, b_down = mlp_whole
    normed_two, pull_two = jax.vjp(
        standardize_features, resid, gain_two.astype(jnp.float32), shift_two.astype(jnp.float32)
    )
    h_two = normed_two.astype(jnp.bfloat16)
    upact = jnp.dot(h_two, w_up, preferred_element_type=jnp.float32) + b_up.astype(jnp.float32)
    activ, gelu_pull = jax.vjp(gelu_apply, upact)
    act_low = activ.astype(jnp.bfloat16)
    output = (
        resid
        + jnp.dot(act_low, w_down, preferred_element_type=jnp.float32)
        + b_down.astype(jnp.float32)
    )
    w_up_back = mlp_whole[2]
    w_down_back = mlp_whole[4]
    out_delta = result_cotangent.reshape(tokens, width)
    out_float = out_delta.astype(jnp.float32)
    downshift_grad = jnp.sum(out_float, 0)
    downmatrix_grad = jnp.einsum(
        "tf,td->fd", act_low, out_delta, preferred_element_type=jnp.float32
    )
    act_delta = jnp.einsum("td,fd->tf", out_delta, w_down_back, preferred_element_type=jnp.float32)
    up_delta = gelu_pull(act_delta)[0].astype(jnp.bfloat16)
    upshift_grad = jnp.sum(up_delta.astype(jnp.float32), 0)
    upmatrix_grad = jnp.einsum("td,tf->df", h_two, up_delta, preferred_element_type=jnp.float32)
    norm_two_delta = jnp.einsum(
        "tf,df->td", up_delta, w_up_back, preferred_element_type=jnp.float32
    )
    resid_part, midgain_grad, midshift_grad = pull_two(norm_two_delta)
    resid_grad = out_float + resid_part
    w_qkv_back = attn_whole[2]
    w_out_back = attn_whole[4]
    proj_delta = resid_grad.astype(jnp.bfloat16)
    outshift_grad = jnp.sum(proj_delta.astype(jnp.float32), 0)
    outmatrix_grad = jnp.einsum(
        "td,te->de", ctx_tok, proj_delta, preferred_element_type=jnp.float32
    )
    ctx_delta = jnp.einsum("te,de->td", proj_delta, w_out_back, preferred_element_type=jnp.float32)
    ctx_heads = lax.all_to_all(
        ctx_delta.astype(jnp.bfloat16), "seq", split_axis=1, concat_axis=0, tiled=True
    )
    qkv_heads_delta = attend_back(heads_in, logsums, ctx_heads)
    qkv_delta = lax.all_to_all(
        qkv_heads_delta, "seq", split_axis=0, concat_axis=2, tiled=True
    ).reshape(tokens, 3 * width)
    qkvshift_grad = jnp.sum(qkv_delta.astype(jnp.float32), 0)
    qkvmatrix_grad = jnp.einsum("td,te->de", h_one, qkv_delta, preferred_element_type=jnp.float32)
    first_norm_gradient = jnp.einsum(
        "te,de->td", qkv_delta, w_qkv_back, preferred_element_type=jnp.float32
    )
    input_portion, prenorm_gain_gradient, prenorm_shift_gradient = first_pullback_step(
        first_norm_gradient
    )
    input_grad = resid_grad + input_portion
    owned = (
        lax.psum_scatter(
            prenorm_gain_gradient.astype(jnp.bfloat16), "dp", scatter_dimension=0, tiled=True
        ).astype(jnp.float32),
        lax.psum_scatter(
            prenorm_shift_gradient.astype(jnp.bfloat16), "dp", scatter_dimension=0, tiled=True
        ).astype(jnp.float32),
        lax.psum_scatter(
            qkvmatrix_grad.astype(jnp.bfloat16), "dp", scatter_dimension=0, tiled=True
        ).astype(jnp.float32),
        lax.psum_scatter(
            qkvshift_grad.astype(jnp.bfloat16), "dp", scatter_dimension=0, tiled=True
        ).astype(jnp.float32),
        lax.psum_scatter(
            outmatrix_grad.astype(jnp.bfloat16), "dp", scatter_dimension=0, tiled=True
        ).astype(jnp.float32),
        lax.psum_scatter(
            outshift_grad.astype(jnp.bfloat16), "dp", scatter_dimension=0, tiled=True
        ).astype(jnp.float32),
        lax.psum_scatter(
            midgain_grad.astype(jnp.bfloat16), "dp", scatter_dimension=0, tiled=True
        ).astype(jnp.float32),
        lax.psum_scatter(
            midshift_grad.astype(jnp.bfloat16), "dp", scatter_dimension=0, tiled=True
        ).astype(jnp.float32),
        lax.psum_scatter(
            upmatrix_grad.astype(jnp.bfloat16), "dp", scatter_dimension=0, tiled=True
        ).astype(jnp.float32),
        lax.psum_scatter(
            upshift_grad.astype(jnp.bfloat16), "dp", scatter_dimension=0, tiled=True
        ).astype(jnp.float32),
        lax.psum_scatter(
            downmatrix_grad.astype(jnp.bfloat16), "dp", scatter_dimension=0, tiled=True
        ).astype(jnp.float32),
        lax.psum_scatter(
            downshift_grad.astype(jnp.bfloat16), "dp", scatter_dimension=0, tiled=True
        ).astype(jnp.float32),
    )
    summed = (
        lax.psum(owned[0].astype(jnp.bfloat16), "seq").astype(jnp.float32),
        lax.psum(owned[1].astype(jnp.bfloat16), "seq").astype(jnp.float32),
        lax.psum(owned[2].astype(jnp.bfloat16), "seq").astype(jnp.float32),
        lax.psum(owned[3].astype(jnp.bfloat16), "seq").astype(jnp.float32),
        lax.psum(owned[4].astype(jnp.bfloat16), "seq").astype(jnp.float32),
        lax.psum(owned[5].astype(jnp.bfloat16), "seq").astype(jnp.float32),
        lax.psum(owned[6].astype(jnp.bfloat16), "seq").astype(jnp.float32),
        lax.psum(owned[7].astype(jnp.bfloat16), "seq").astype(jnp.float32),
        lax.psum(owned[8].astype(jnp.bfloat16), "seq").astype(jnp.float32),
        lax.psum(owned[9].astype(jnp.bfloat16), "seq").astype(jnp.float32),
        lax.psum(owned[10].astype(jnp.bfloat16), "seq").astype(jnp.float32),
        lax.psum(owned[11].astype(jnp.bfloat16), "seq").astype(jnp.float32),
    )
    return (output.reshape(1, tokens, width), input_grad.reshape(1, tokens, width)) + tuple(summed)


def solution(mesh):
    in_specs = (
        P("dp", "seq", None),
        P("dp", "seq", None),
        P("dp"),
        P("dp"),
        P("dp", None),
        P("dp"),
        P("dp", None),
        P("dp"),
        P("dp"),
        P("dp"),
        P("dp", None),
        P("dp"),
        P("dp", None),
        P("dp"),
    )
    out_specs = (
        P("dp", "seq", None),
        P("dp", "seq", None),
        P("dp"),
        P("dp"),
        P("dp", None),
        P("dp"),
        P("dp", None),
        P("dp"),
        P("dp"),
        P("dp"),
        P("dp", None),
        P("dp"),
        P("dp", None),
        P("dp"),
    )
    return jax.shard_map(local, mesh=mesh, in_specs=in_specs, out_specs=out_specs, check_vma=False)
```

profile of v0, /device:TPU:0, one launch (start us, length us, event | category | flops | bytes accessed | tf_op | source)
XLA Modules:
  0.0 885.2 jit_solution(8268792377853968810)
XLA Ops:
  17.1 64.3 %all-reduce.18 = (bf16[3072]{0:T(1024)(128)(2,1)S(1)}, bf16[1024]{0:T(1024)(128)(2,1)S(1)}, bf16[1024]{0:T(1024)(128)(2,1)S(1)}, bf16[1024]{0:T(1024)(128)(2,1)S...) all-reduce(bf16[3072]{0:T(1024)(128)(2,1)S(1)} %dynamic-update-slic, ...), channel_id=1, replica_groups=mesh['dp'=16,'seq'=2] {'dp'}, use_global_device_ids=true, to_apply=%add.4 | all-reduce | flops 8192 | bytes 32768
  84.4 7.8 add_convert_fusion
  92.2 3.2 copy.238
  95.4 4.7 copy.239
  100.2 5.7 all-to-all-start
  106.5 17.2 %all-gather = bf16[16,1,256]{2,1,0:T(2,128)(2,1)S(1)} all-gather(bf16[1,1,256]{2,1,0:T(2,128)(2,1)S(1)} %reshape.755), channel_id=1, replica_groups=mesh['dp'=16,'seq'=2] {'dp'}, dimensions={0}, use_global_device_ids=true | all-gather | bytes 8704 | tf_op jit(solution)/shard_map/all_gather | solution.py:176
  123.8 25.4 %all-to-all-done = bf16[512,3,1024]{0,1,2:T(4,128)(2,1)} async-done(((bf16[512,3,1024]{0,1,2:T(4,128)(2,1)}), bf16[512,3,1024]{0,1,2:T(4,128)(2,1)}, u32[]{:S(2)}, u32[]{:S(2)}) %all-to-all-start) | async-done | bytes 3145760 | tf_op jit(solution)/shard_map/all_to_all | solution.py:162
  149.2 4.6 copy.240
  153.8 3.4 copy.241
  186.2 2.3 copy.242
  188.5 4.7 all-to-all-start.1
  193.4 9.2 %all-to-all-done.1 = bf16[2,512,512]{1,2,0:T(8,128)(2,1)} async-done(((bf16[2,512,512]{1,2,0:T(8,128)(2,1)}), bf16[2,512,512]{1,2,0:T(8,128)(2,1)}, u32[]{:S(2)}, u32[]{:S(2)}) %all-to-all-start.1) | async-done | bytes 1048608 | tf_op jit(solution)/shard_map/all_to_all | solution.py:164
  202.6 3.6 fusion.481
  207.9 12.0 %fusion.459 = f32[512,4096]{1,0:T(8,128)} fusion(bf16[1024,4096]{1,0:T(8,128)(2,1)} %all-gather.10.cloned.1.call-done, f32[512,1024]{1,0:T(8,128)} %copy-done.20, f32[1024]{0:T(1024)S(1)} %convert_element_type.583, f32[1024]{0:T(1024)S(1)} %convert_element_type.582, f32[512]{0:T(512)S(1)} %fusion.393, f32[512]{0:T(512)S(1)} %broadcast_multiply_fusion), kind=kOutput, calls=%fused_computation.672 | convolution fusion | flops 4297588736 | bytes 18886656 | tf_op jit(solution)/shard_map/dot_general | solution.py:185
  219.9 49.0 %all-gather.12.cloned.1.call-done = bf16[4096,1024]{1,0:T(8,128)(2,1)} async-done(((bf16[256,1024]{1,0:T(8,128)(2,1)}), bf16[4096,1024]{1,0:T(8,128)(2,1)}) %all-gather.12.cloned.1.call-update) | async-done | bytes 8388624 | tf_op jit(solution)/shard_map/all_gather | solution.py:177
  268.9 15.3 %fusion.482 = (bf16[4096]{0:T(1024)(128)(2,1)}, bf16[512,4096]{1,0:T(8,128)(2,1)}) fusion(f32[512,4096]{1,0:T(8,128)} %fusion.459, f32[4096]{0:T(1024)S(1)} %bitcast.653, bf16[4096,1024]{1,0:T(8,128)(2,1)} %all-gather.12.cloned.1.call-done, bf16[1,512,1024]{2,1,0:T(8,128)(2,1)} %param.27), kind=kOutput, calls=%fused_computation.694 | convolution fusion | flops 4341100544 | bytes 22044672 | tf_op jit(solution)/shard_map/td,fd->tf/dot_general | solution.py:201
  284.2 8.1 multiply_reduce_fusion
  297.6 4.4 all-to-all-start.2
  302.1 4.2 convolution_convert_fusion.3
  306.7 9.7 %all-to-all-done.2 = bf16[512,2,512]{2,0,1:T(8,128)(2,1)} async-done(((bf16[512,2,512]{2,0,1:T(8,128)(2,1)}), bf16[512,2,512]{2,0,1:T(8,128)(2,1)}, u32[]{:S(2)}, u32[]{:S(2)}) %all-to-all-start.2) | async-done | bytes 1048608 | tf_op jit(solution)/shard_map/all_to_all | solution.py:218
  316.4 2.0 fusion.162
  323.2 1.9 fusion.70
  325.1 2.1 multiply_reduce_fusion.7
  329.2 2.1 multiply_reduce_fusion.6
  333.2 2.1 multiply_reduce_fusion.5
  337.2 3.4 multiply_reduce_fusion.4
  342.5 3.3 multiply_reduce_fusion.3
  345.8 1.9 fusion.60
  347.8 3.3 multiply_reduce_fusion.2
  353.0 2.1 multiply_reduce_fusion.8
  356.6 3.0 fusion.124
  360.9 2.5 multiply_reduce_fusion.17
  365.1 2.5 multiply_reduce_fusion.16
  369.2 2.5 multiply_reduce_fusion.15
  378.0 2.6 convolution_add_fusion.2
  382.2 2.9 convolution_add_fusion.1
  385.1 2.5 multiply_reduce_fusion.11
  387.6 2.9 convolution_add_fusion
  392.0 2.7 convolution_add_fusion.13
  394.7 2.8 convolution_add_fusion.27
  397.8 2.8 convolution_add_fusion.12
  416.0 2.1 fusion.168
  418.7 2.1 fusion.169
  421.2 2.1 fusion.170
  423.3 2.0 multiply_reduce_fusion.1
  435.5 3.9 fusion.42
  439.4 4.4 fusion.41
  445.4 5.7 copy.292
  451.1 51.4 %all_to_all.65 = bf16[1024,3,512]{2,1,0:T(4,128)(2,1)S(1)} all-to-all(bf16[1024,3,512]{2,1,0:T(4,128)(2,1)} %copy.292), channel_id=1, replica_groups=mesh['dp'=16,'seq'=2] {'seq'}, dimensions={0} | all-to-all | bytes 6291456 | tf_op jit(solution)/shard_map/all_to_all | solution.py:222
  502.5 2.4 bitcast_reduce_fusion
  504.9 4.8 copy.294
  509.8 7.8 convolution_convert_fusion.2
  518.8 13.6 %convolution_convert_fusion = bf16[4096,1024]{1,0:T(8,128)(2,1)} fusion(bf16[1,512,1024]{2,1,0:T(8,128)(2,1)S(1)} %copy-done.40, f32[512,4096]{1,0:T(8,128)} %fusion.459, f32[4096]{0:T(1024)S(1)} %bitcast.654), kind=kOutput, calls=%fused_computation.10 | convolution fusion | flops 4320133120 | bytes 17842176 | tf_op jit(solution)/shard_map/tf,td->fd/dot_general | solution.py:198
  534.2 9.6 %convolution_convert_fusion.1 = bf16[1024,4096]{1,0:T(8,128)(2,1)} fusion(bf16[512,4096]{1,0:T(8,128)(2,1)} %get-tuple-element.189, f32[512,1024]{1,0:T(8,128)S(1)} %copy-done.22, f32[1024]{0:T(1024)S(1)} %copy-done.77, f32[1024]{0:T(1024)S(1)} %convert_element_type.582, f32[512]{0:T(512)S(1)} %fusion.393, f32[512]{0:T(512)S(1)} %broadcast_multiply_fusion), kind=kOutput, calls=%fused_computation.11 | convolution fusion | flops 4301783040 | bytes 14692352 | tf_op jit(solution)/shard_map/td,tf->df/dot_general | solution.py:204
  546.3 6.9 fusion.460
  555.6 59.8 %all-reduce.17 = (bf16[1024]{0:T(1024)(128)(2,1)S(1)}, bf16[1024]{0:T(1024)(128)(2,1)S(1)}, bf16[1024]{0:T(1024)(128)(2,1)S(1)}, bf16[3072]{0:T(1024)(128)(2,1)S...) all-reduce(bf16[1024]{0:T(1024)(128)(2,1)S(1)} %dynamic-update-slic, ...), channel_id=1, replica_groups=mesh['dp'=16,'seq'=2] {'dp'}, use_global_device_ids=true, to_apply=%add.8 | all-reduce | flops 14336 | bytes 57344
  616.0 4.9 all-reduce.19
  625.2 4.2 add_bitcast_fusion
  629.4 79.4 %reduce-scatter.11.cloned.1.call-done = bf16[256,1024]{1,0:T(8,128)(2,1)} async-done(((bf16[4096,1024]{1,0:T(8,128)(2,1)}), bf16[256,1024]{1,0:T(8,128)(2,1)}) %reduce-scatter.11.cloned.1.call-update) | async-done | bytes 524304 | tf_op jit(solution)/shard_map/reduce_scatter | solution.py:265
  708.8 108.6 %reduce-scatter.9.cloned.1.call-done = bf16[64,4096]{1,0:T(8,128)(2,1)} async-done(((bf16[1024,4096]{1,0:T(8,128)(2,1)}), bf16[64,4096]{1,0:T(8,128)(2,1)}) %reduce-scatter.9.cloned.1.call-update) | async-done | bytes 524304 | tf_op jit(solution)/shard_map/reduce_scatter | solution.py:259
  817.4 13.2 %add_bitcast_fusion.1 = f32[1,512,1024]{2,1,0:T(8,128)} fusion(f32[512,1024]{1,0:T(8,128)} %copy-done.20, bf16[4096,1024]{1,0:T(8,128)(2,1)} %all-gather.12.cloned.1.call-done, f32[1024]{0:T(1024)S(1)} %convert_element_type.587, f32[512,4096]{1,0:T(8,128)} %fusion.459, f32[4096]{0:T(1024)S(1)} %bitcast.655), kind=kOutput, calls=%fused_computation.68 | convolution fusion | flops 4316987392 | bytes 20992000 | tf_op jit(solution)/shard_map/dot_general | solution.py:190
  830.6 41.1 %all-reduce.23.cloned.1.call-done = (bf16[64,3072]{1,0:T(8,128)(2,1)}, bf16[64,1024]{1,0:T(8,128)(2,1)}, bf16[64,4096]{1,0:T(8,128)(2,1)}, bf16[256,1024]{1,0:T(8,128)(2,1)}) async-done(((bf16[64,3072]{1,0:T(8,128)(2,1)}, bf16[64,1024]{1,0:T(8,128)(2,1)}, bf16[64,4096]{1,0:T(8,128)(2,1)}, bf16[256,1024]{1,0:T(8,128)(2,1)}), (bf16[64,3072]{1,0:T(8,128)(2,1)}, bf16[64,1024]{1,0:T(8,128)(2,1)}, ...) | async-done | bytes 1572880 | tf_op jit(solution)/shard_map/psum | solution.py:275
  873.3 1.9 convert_element_type.631
  875.3 2.1 convert_element_type.641
  (378 shorter events, 119.7 us)
Async XLA Ops:
  7.2 75.6 %copy-start.16 = (bf16[1,512,1024]{2,1,0:T(8,128)(2,1)S(1)}, bf16[1,512,1024]{2,1,0:T(8,128)(2,1)}, u32[]{:S(2)}) copy-start(bf16[1,512,1024]{2,1,0:T(8,128)(2,1)} %param.26) | copy-start | bytes 3145732
  7.2 76.7 %all-gather.6.cloned.1.call-start = ((), (), s32[]{:S(2)}) async-start(), calls=%async_computation.8 | async-start | bytes 6684672 | tf_op jit(solution)/shard_map/all_gather | solution.py:150
  7.9 185.5 %all-gather.8.cloned.1.call-start = ((), (), s32[]{:S(2)}) async-start(), calls=%async_computation.9 | async-start | bytes 2228224 | tf_op jit(solution)/shard_map/all_gather | solution.py:152
  8.7 199.2 %all-gather.10.cloned.1.call-start = ((), (), s32[]{:S(2)}) async-start(), calls=%async_computation.10 | async-start | bytes 8912896 | tf_op jit(solution)/shard_map/all_gather | solution.py:175
  81.3 2.5 copy-start.62
  81.3 2.5 copy-start.74
  100.2 6.3 copy-start.81
  100.2 49.0 %all-to-all-start = ((bf16[512,3,1024]{0,1,2:T(4,128)(2,1)}), bf16[512,3,1024]{0,1,2:T(4,128)(2,1)}, u32[]{:S(2)}, u32[]{:S(2)}) async-start(bf16[512,3,1024]{0,1,2:T(4,128)(2,1)} %copy.239), calls=%async_computation | async-start | bytes 8388608 | tf_op jit(solution)/shard_map/all_to_all | solution.py:162
  105.9 163.0 %all-gather.12.cloned.1.call-start = ((), (), s32[]{:S(2)}) async-start(), calls=%async_computation.11 | async-start | bytes 8912896 | tf_op jit(solution)/shard_map/all_gather | solution.py:177
  106.5 101.4 %copy-start.76 = (f32[1024]{0:T(1024)}, f32[1024]{0:T(1024)S(1)}, u32[]{:S(2)}) copy-start(f32[1024]{0:T(1024)S(1)} %convert_element_type.583) | copy-start | bytes 12292
  157.8 17.3 %copy-start.37 = (f32[512,512]{0,1:T(8,128)}, f32[512,512]{0,1:T(8,128)S(1)}, u32[]{:S(2)}) copy-start(f32[512,512]{0,1:T(8,128)S(1)} %get-tuple-element.139) | copy-start | bytes 3145732
  158.3 17.3 %copy-start.35 = (f32[512,512]{0,1:T(8,128)}, f32[512,512]{0,1:T(8,128)S(1)}, u32[]{:S(2)}) copy-start(f32[512,512]{0,1:T(8,128)S(1)} %get-tuple-element.141) | copy-start | bytes 3145732
  159.2 20.4 %copy-start.6 = (f32[512,1024]{1,0:T(8,128)}, f32[512,1024]{1,0:T(8,128)S(1)}, u32[]{:S(2)}) copy-start(f32[512,1024]{1,0:T(8,128)S(1)} %get-tuple-element.123) | copy-start | bytes 6291460
  160.1 20.3 %copy-start.4 = (f32[512,1024]{1,0:T(8,128)}, f32[512,1024]{1,0:T(8,128)S(1)}, u32[]{:S(2)}) copy-start(f32[512,1024]{1,0:T(8,128)S(1)} %get-tuple-element.125) | copy-start | bytes 6291460
  160.6 15.6 %copy-start.33 = (f32[512,512]{0,1:T(8,128)}, f32[512,512]{0,1:T(8,128)S(1)}, u32[]{:S(2)}) copy-start(f32[512,512]{0,1:T(8,128)S(1)} %get-tuple-element.143) | copy-start | bytes 3145732
  161.5 19.7 %copy-start.2 = (f32[512,1024]{1,0:T(8,128)}, f32[512,1024]{1,0:T(8,128)S(1)}, u32[]{:S(2)}) copy-start(f32[512,1024]{1,0:T(8,128)S(1)} %get-tuple-element.127) | copy-start | bytes 6291460
  162.0 14.7 %copy-start.31 = (f32[512,512]{0,1:T(8,128)}, f32[512,512]{0,1:T(8,128)S(1)}, u32[]{:S(2)}) copy-start(f32[512,512]{0,1:T(8,128)S(1)} %get-tuple-element.145) | copy-start | bytes 3145732
  162.5 14.7 %copy-start.29 = (f32[512,512]{0,1:T(8,128)}, f32[512,512]{0,1:T(8,128)S(1)}, u32[]{:S(2)}) copy-start(f32[512,512]{0,1:T(8,128)S(1)} %get-tuple-element.147) | copy-start | bytes 3145732
  163.0 14.7 %copy-start.27 = (f32[512,512]{0,1:T(8,128)}, f32[512,512]{0,1:T(8,128)S(1)}, u32[]{:S(2)}) copy-start(f32[512,512]{0,1:T(8,128)S(1)} %get-tuple-element.149) | copy-start | bytes 3145732
  163.5 14.7 %copy-start.25 = (f32[512,512]{0,1:T(8,128)}, f32[512,512]{0,1:T(8,128)S(1)}, u32[]{:S(2)}) copy-start(f32[512,512]{0,1:T(8,128)S(1)} %get-tuple-element.151) | copy-start | bytes 3145732
  164.0 10.6 %copy-start.23 = (f32[512,512]{0,1:T(8,128)}, f32[512,512]{0,1:T(8,128)S(1)}, u32[]{:S(2)}) copy-start(f32[512,512]{0,1:T(8,128)S(1)} %get-tuple-element.137) | copy-start | bytes 3145732
  168.0 13.9 %copy-start.12 = (f32[512,1024]{1,0:T(8,128)}, f32[512,1024]{1,0:T(8,128)S(1)}, u32[]{:S(2)}) copy-start(f32[512,1024]{1,0:T(8,128)S(1)} %get-tuple-element.129) | copy-start | bytes 6291460
  169.4 13.3 %copy-start.10 = (f32[512,1024]{1,0:T(8,128)}, f32[512,1024]{1,0:T(8,128)S(1)}, u32[]{:S(2)}) copy-start(f32[512,1024]{1,0:T(8,128)S(1)} %get-tuple-element.131) | copy-start | bytes 6291460
  170.8 12.7 %copy-start.8 = (f32[512,1024]{1,0:T(8,128)}, f32[512,1024]{1,0:T(8,128)S(1)}, u32[]{:S(2)}) copy-start(f32[512,1024]{1,0:T(8,128)S(1)} %get-tuple-element.133) | copy-start | bytes 6291460
  172.2 12.1 %copy-start = (f32[512,1024]{1,0:T(8,128)}, f32[512,1024]{1,0:T(8,128)S(1)}, u32[]{:S(2)}) copy-start(f32[512,1024]{1,0:T(8,128)S(1)} %get-tuple-element.135) | copy-start | bytes 6291460
  174.0 4.7 copy-start.14
  188.5 14.2 %all-to-all-start.1 = ((bf16[2,512,512]{1,2,0:T(8,128)(2,1)}), bf16[2,512,512]{1,2,0:T(8,128)(2,1)}, u32[]{:S(2)}, u32[]{:S(2)}) async-start(bf16[2,512,512]{1,2,0:T(8,128)(2,1)} %copy.242), calls=%async_computation.1 | async-start | bytes 2097152 | tf_op jit(solution)/shard_map/all_to_all | solution.py:164
  268.8 15.3 %copy-start.21 = (f32[512,1024]{1,0:T(8,128)S(1)}, f32[512,1024]{1,0:T(8,128)}, u32[]{:S(2)}) copy-start(f32[512,1024]{1,0:T(8,128)} %copy-done.20) | copy-start | bytes 6291460
  268.9 15.3 %copy-start.80 = (bf16[1024,4096]{1,0:T(8,128)(2,1)S(1)}, bf16[1024,4096]{1,0:T(8,128)(2,1)}, u32[]{:S(2)}) copy-start(bf16[1024,4096]{1,0:T(8,128)(2,1)} %all-gather.10.cloned.1.call-done) | copy-start | bytes 25165828
  294.4 2.2 copy-start.60
  297.6 18.8 %all-to-all-start.2 = ((bf16[512,2,512]{2,0,1:T(8,128)(2,1)}), bf16[512,2,512]{2,0,1:T(8,128)(2,1)}, u32[]{:S(2)}, u32[]{:S(2)}) async-start(bf16[512,2,512]{2,0,1:T(8,128)(2,1)} %bitcast.646), calls=%async_computation.2 | async-start | bytes 2097152 | tf_op jit(solution)/shard_map/all_to_all | solution.py:218
  302.0 327.4 %reduce-scatter.7.cloned.1.call-start = ((), (), s32[]{:S(2)}) async-start(), calls=%async_computation.13 | async-start | bytes 2228224 | tf_op jit(solution)/shard_map/reduce_scatter | solution.py:247
  306.3 323.1 %reduce-scatter.5.cloned.1.call-start = ((), (), s32[]{:S(2)}) async-start(), calls=%async_computation.12 | async-start | bytes 6684672 | tf_op jit(solution)/shard_map/reduce_scatter | solution.py:241
  320.2 3.0 copy-start.7
  325.1 2.1 copy-start.5
  337.2 3.4 copy-start.11
  342.5 3.4 copy-start.9
  347.8 3.3 copy-start.15
  356.6 3.1 copy-start.57
  378.0 2.6 copy-start.28
  382.2 3.0 copy-start.26
  394.7 2.8 copy-start.49
  397.8 2.8 copy-start.54
  416.0 2.1 copy-start.45
  435.5 3.9 copy-start.43
  439.4 4.4 copy-start.50
  504.9 4.9 copy-start.17
  504.9 4.9 copy-start.63
  504.9 4.8 copy-start.65
  504.9 4.8 copy-start.71
  504.9 4.8 copy-start.75
  517.6 191.2 %reduce-scatter.11.cloned.1.call-start = ((), (), s32[]{:S(2)}) async-start(), calls=%async_computation.15 | async-start | bytes 8912896 | tf_op jit(solution)/shard_map/reduce_scatter | solution.py:265
  532.4 284.9 %reduce-scatter.9.cloned.1.call-start = ((), (), s32[]{:S(2)}) async-start(), calls=%async_computation.14 | async-start | bytes 8912896 | tf_op jit(solution)/shard_map/reduce_scatter | solution.py:259
  543.7 2.1 copy-start.41
  543.7 2.3 copy-start.82
  543.7 327.9 %all-reduce.23.cloned.1.call-start = ((), (), s32[]{:S(2)}) async-start(), calls=%async_computation.16 | async-start | bytes 3145728 | tf_op jit(solution)/shard_map/psum | solution.py:275
  546.3 7.0 copy-start.69
  553.2 2.3 copy-start.72
  553.2 2.3 copy-start.73
  553.2 2.3 copy-start.78
  553.2 2.3 copy-start.79
  553.3 71.9 %copy-start.19 = (f32[512,1024]{1,0:T(8,128)S(1)}, f32[512,1024]{1,0:T(8,128)}, u32[]{:S(2)}) copy-start(f32[512,1024]{1,0:T(8,128)} %copy-done.18) | copy-start | bytes 6291460
  553.3 71.9 %copy-start.67 = (f32[512]{0:T(512)S(1)}, f32[512]{0:T(512)}, u32[]{:S(2)}) copy-start(f32[512]{0:T(512)} %copy-done.66) | copy-start | bytes 6148
  871.7 5.7 copy-start.61
  (31 other events, 46.0 us)
Sparse Core Ops, SparseCore 0:
  10.3 65.1 all-gather.5
  77.7 40.0 all-gather.7
  119.9 73.6 all-gather.9
  195.7 73.1 all-gather.11
  306.4 60.2 reduce-scatter.6
  517.7 83.3 reduce-scatter.4
  605.2 103.5 reduce-scatter.10
  712.9 104.4 reduce-scatter.8
  819.8 51.7 all-reduce.22
where the time goes:
time: 895 us; the launch traced here: 885 us
  waiting for transfers between devices  325 us (36%)
  matrix products  239 us (27%)
  blocking collectives  198 us (22%)
  local copies, waits for them, and re-layouts  50.6 us (6%)
  other arithmetic  38.9 us (4%)
  between operations  18.9 us (2%)
  starting transfers between devices  15.7 us (2%)
    unnamed x2, blocking collectives  124 us
    reduce_scatter x1, waiting for transfers between devices, local(): lax.psum_scatter(upmatrix_grad.astype(jnp.bfloat16), 'dp', scatter_dimens...  109 us
    reduce_scatter x1, waiting for transfers between devices, local(): lax.psum_scatter(downmatrix_grad.astype(jnp.bfloat16), 'dp', scatter_dime...  79.4 us
    all_to_all x1, blocking collectives, local(): lax.all_to_all(qkv_heads_delta, 'seq', split_axis=0, concat_axis=2, tiled...  51.4 us
    all_gather x1, waiting for transfers between devices, local(): lax.all_gather(contract_projection_matrix, 'dp', axis=0, tiled=True)  49 us
    psum x1, waiting for transfers between devices, local(): lax.psum(owned[2].astype(jnp.bfloat16), 'seq').astype(jnp.float32)  41.1 us
    dot_general x16, matrix products, attend_back(): lax.dot_general(gblock, valuepart * mask, (((1,), (1,)), ((), ())), prefe...  36.6 us
    dot_general x16, matrix products, attend_back(): lax.dot_general(probab.astype(jnp.bfloat16), gblock * mask, (((0,), (0,))...  34.2 us
  transfers between devices with their start and end apart: 12, of which 7 were waited for; matrix products, arithmetic and copies ran while one was open for 32% of the time, Pallas kernels for 0%

commit v1 on v0

v1 whole, which is shorter than its diff:
```python
import functools

import jax
import jax.numpy as jnp
from jax import lax
from jax.experimental import pallas as pl
from jax.experimental.pallas import tpu as pltpu
from jax.sharding import PartitionSpec as P

HD = 64
LANES = 128
EPS = 1e-05
NEG = -1e30
FACTOR = HD ** (-0.5)
VMEM_BYTES = 40 * 1024 * 1024


def standardize_features(values, gain, shift):
    center = values - jnp.mean(values, -1, keepdims=True)
    spread = jnp.mean(center * center, -1, keepdims=True)
    return center * lax.rsqrt(spread + EPS) * gain + shift


def gelu_apply(values):
    return jax.nn.gelu(values, approximate=True)


def dot_nt(left, right):
    return lax.dot_general(
        left, right, (((1,), (1,)), ((), ())), preferred_element_type=jnp.float32
    )


def dot_tn(left, right):
    return lax.dot_general(
        left, right, (((0,), (0,)), ((), ())), preferred_element_type=jnp.float32
    )


def dot_nn(left, right):
    return jnp.dot(left, right, preferred_element_type=jnp.float32)


def head_mask(head, dtype):
    lane = lax.broadcasted_iota(jnp.int32, (1, LANES), 1)
    return (lane // HD == head).astype(dtype)


def row_step(rows):
    return min(256, rows)


def causal(scores, start):
    query_pos = start + lax.broadcasted_iota(jnp.int32, scores.shape, 0)
    key_pos = lax.broadcasted_iota(jnp.int32, scores.shape, 1)
    return jnp.where(key_pos <= query_pos, scores, NEG)


def before(scores, limit):
    key_pos = lax.broadcasted_iota(jnp.int32, scores.shape, 1)
    return jnp.where(key_pos < limit, scores, NEG)


def forward_kernel(limit_ref, q_ref, k_ref, v_ref, kr_ref, vr_ref, ctx_ref, lse_ref):
    rows = q_ref.shape[0]
    step = row_step(rows)
    limit = limit_ref[0]
    lane = lax.broadcasted_iota(jnp.int32, (step, LANES), 1)
    for start in range(0, rows, step):
        end = start + step
        context = jnp.zeros((step, LANES), jnp.float32)
        sums = []
        for head in range(2):
            mask = head_mask(head, jnp.bfloat16)
            queries = q_ref[start:end] * mask
            own = causal(dot_nt(queries, k_ref[:end]) * FACTOR, start)
            far = before(dot_nt(queries, kr_ref[...]) * FACTOR, limit)
            highest = jnp.maximum(
                jnp.max(own, -1, keepdims=True), jnp.max(far, -1, keepdims=True)
            )
            own = jnp.exp(own - highest)
            far = jnp.exp(far - highest)
            total = jnp.sum(own, -1, keepdims=True) + jnp.sum(far, -1, keepdims=True)
            inverse = 1.0 / total
            context = context + dot_nn((own * inverse).astype(jnp.bfloat16), v_ref[:end] * mask)
            context = context + dot_nn((far * inverse).astype(jnp.bfloat16), vr_ref[...] * mask)
            sums.append(highest + jnp.log(total))
        ctx_ref[start:end] = context.astype(jnp.bfloat16)
        lse_ref[start:end] = jnp.where(lane < HD, sums[0], sums[1])


def back_block(q_ref, g_ref, ctx_ref, lse_ref, keys, values, start, end, head, cut):
    mask = head_mask(head, jnp.bfloat16)
    queries = q_ref[start:end] * mask
    grads = g_ref[start:end] * mask
    inner = jnp.sum(
        grads.astype(jnp.float32) * ctx_ref[start:end].astype(jnp.float32), -1, keepdims=True
    )
    logsum = lse_ref[start:end, head * HD : head * HD + 1]
    probab = jnp.exp(cut(dot_nt(queries, keys) * FACTOR) - logsum)
    delta = (probab * (dot_nt(grads, values) - inner)).astype(jnp.bfloat16)
    return (
        dot_nn(delta, keys * mask) * FACTOR,
        dot_tn(delta, queries) * FACTOR,
        dot_tn(probab.astype(jnp.bfloat16), grads),
    )


def back_far_kernel(
    limit_ref, q_ref, g_ref, ctx_ref, lse_ref, kr_ref, vr_ref, dq_ref, dk_ref, dv_ref
):
    rows = q_ref.shape[0]
    step = row_step(rows)
    limit = limit_ref[0]
    dk = jnp.zeros(kr_ref.shape, jnp.float32)
    dv = jnp.zeros(kr_ref.shape, jnp.float32)
    for start in range(0, rows, step):
        end = start + step
        dq = jnp.zeros((step, LANES), jnp.float32)
        for head in range(2):
            one, two, three = back_block(
                q_ref, g_ref, ctx_ref, lse_ref, kr_ref[...], vr_ref[...], start, end, head,
                lambda s: before(s, limit),
            )
            dq, dk, dv = dq + one, dk + two, dv + three
        dq_ref[start:end] = dq
    dk_ref[...] = dk.astype(jnp.bfloat16)
    dv_ref[...] = dv.astype(jnp.bfloat16)


def back_own_kernel(
    q_ref, g_ref, ctx_ref, lse_ref, k_ref, v_ref, dqfar_ref, dq_ref, dk_ref, dv_ref
):
    rows = q_ref.shape[0]
    step = row_step(rows)
    dk_ref[...] = jnp.zeros(dk_ref.shape, jnp.float32)
    dv_ref[...] = jnp.zeros(dv_ref.shape, jnp.float32)
    for start in range(0, rows, step):
        end = start + step
        dq = dqfar_ref[start:end]
        for head in range(2):
            one, two, three = back_block(
                q_ref, g_ref, ctx_ref, lse_ref, k_ref[:end], v_ref[:end], start, end, head,
                lambda s: causal(s, start),
            )
            dq = dq + one
            dk_ref[:end] += two
            dv_ref[:end] += three
        dq_ref[start:end] = dq.astype(jnp.bfloat16)


def pair_spec(rows, base):
    return pl.BlockSpec((rows, LANES), lambda pair: (0, base + pair))


def cost(rows, keys, width, products):
    return pl.CostEstimate(
        flops=4 * 2 * products * rows * keys * width,
        bytes_accessed=2 * width * (4 * rows + 4 * keys),
        transcendentals=rows * keys * width // HD,
    )


LIMIT_SPEC = pl.BlockSpec(memory_space=pltpu.SMEM)
PARAMS = pltpu.CompilerParams(vmem_limit_bytes=VMEM_BYTES)


def attend(limit, queries, keyvals, far):
    rows, width = queries.shape
    extent = far.shape[0]
    pairs = width // LANES
    return pl.pallas_call(
        forward_kernel,
        grid=(pairs,),
        in_specs=[
            LIMIT_SPEC,
            pair_spec(rows, 0),
            pair_spec(rows, 0),
            pair_spec(rows, pairs),
            pair_spec(extent, 0),
            pair_spec(extent, pairs),
        ],
        out_specs=[pair_spec(rows, 0), pair_spec(rows, 0)],
        out_shape=[
            jax.ShapeDtypeStruct((rows, width), jnp.bfloat16),
            jax.ShapeDtypeStruct((rows, width), jnp.float32),
        ],
        compiler_params=PARAMS,
        cost_estimate=cost(rows, rows + extent, width, 2),
        name="attend",
    )(limit, queries, keyvals, keyvals, far, far)


def attend_back_far(limit, queries, grads, context, logsum, far):
    rows, width = queries.shape
    extent = far.shape[0]
    pairs = width // LANES
    return pl.pallas_call(
        back_far_kernel,
        grid=(pairs,),
        in_specs=[LIMIT_SPEC]
        + [pair_spec(rows, 0)] * 4
        + [pair_spec(extent, 0), pair_spec(extent, pairs)],
        out_specs=[pair_spec(rows, 0), pair_spec(extent, 0), pair_spec(extent, 0)],
        out_shape=[
            jax.ShapeDtypeStruct((rows, width), jnp.float32),
            jax.ShapeDtypeStruct((extent, width), jnp.bfloat16),
            jax.ShapeDtypeStruct((extent, width), jnp.bfloat16),
        ],
        compiler_params=PARAMS,
        cost_estimate=cost(rows, extent, width, 5),
        name="attend_back_far",
    )(limit, queries, grads, context, logsum, far, far)


def attend_back_own(queries, grads, context, logsum, keyvals, dq_far):
    rows, width = queries.shape
    pairs = width // LANES
    return pl.pallas_call(
        back_own_kernel,
        grid=(pairs,),
        in_specs=[pair_spec(rows, 0)] * 4
        + [pair_spec(rows, 0), pair_spec(rows, pairs), pair_spec(rows, 0)],
        out_specs=[pair_spec(rows, 0)] * 3,
        out_shape=[
            jax.ShapeDtypeStruct((rows, width), jnp.bfloat16),
            jax.ShapeDtypeStruct((rows, width), jnp.float32),
            jax.ShapeDtypeStruct((rows, width), jnp.float32),
        ],
        compiler_params=PARAMS,
        cost_estimate=cost(rows, rows, width, 5),
        name="attend_back_own",
    )(queries, grads, context, logsum, keyvals, keyvals, dq_far)


def pack_rows(pieces, rows):
    joined = jnp.concatenate(pieces, -1)
    spare = rows * LANES - joined.shape[-1]
    padded = jnp.pad(joined, ((0, 0), (0, spare)))
    return padded.reshape(joined.shape[0] * rows, LANES)


def unpack_rows(packed, shards, lengths):
    flat = packed.reshape(shards, -1)
    pieces, at = [], 0
    for length in lengths:
        pieces.append(flat[:, at : at + length].reshape(-1))
        at += length
    return pieces


def swap_sum(value, ranks):
    if ranks == 2:
        other = lax.ppermute(value, "seq", [(0, 1), (1, 0)])
        return value.astype(jnp.float32) + other.astype(jnp.float32)
    return lax.psum(value, "seq").astype(jnp.float32)


def local(
    block_entry_tokens,
    result_cotangent,
    leading_scale_factor,
    leading_bias_vector,
    query_key_value_matrix,
    query_key_value_bias,
    attention_exit_matrix,
    attention_exit_bias,
    latter_scale_factor,
    latter_bias_vector,
    expand_projection_matrix,
    expand_projection_offset,
    contract_projection_matrix,
    contract_projection_offset,
    shards,
    ranks,
):
    f32, bf16 = jnp.float32, jnp.bfloat16
    hidden = block_entry_tokens.reshape(-1, block_entry_tokens.shape[-1]).astype(f32)
    tokens, width = hidden.shape
    place = lax.axis_index("seq")
    limit = (place * tokens).astype(jnp.int32).reshape(1)
    vectors = (
        leading_scale_factor,
        leading_bias_vector,
        query_key_value_bias,
        attention_exit_bias,
        latter_scale_factor,
        latter_bias_vector,
        expand_projection_offset,
        contract_projection_offset,
    )
    lengths = [vector.shape[0] for vector in vectors]
    rows = query_key_value_matrix.shape[0]
    small = pack_rows([vector[None] for vector in vectors], rows)
    attn_whole = lax.all_gather(
        jnp.concatenate([query_key_value_matrix, attention_exit_matrix, small], 1),
        "dp",
        axis=0,
        tiled=True,
    )
    w_up = lax.all_gather(expand_projection_matrix, "dp", axis=0, tiled=True)
    w_down = lax.all_gather(contract_projection_matrix, "dp", axis=0, tiled=True)
    w_q = attn_whole[:, :width]
    w_kv = attn_whole[:, width : 3 * width]
    w_qkv = attn_whole[:, : 3 * width]
    w_out = attn_whole[:, 3 * width : 4 * width]
    gain_one, shift_one, b_qkv, b_out, gain_two, shift_two, b_up, b_down = (
        vector.astype(f32) for vector in unpack_rows(attn_whole[:, 4 * width :], shards, lengths)
    )

    normed_one, pull_one = jax.vjp(standardize_features, hidden, gain_one, shift_one)
    h_one = normed_one.astype(bf16)
    keyvals = (dot_nn(h_one, w_kv) + b_qkv[width:]).astype(bf16)
    if ranks == 2:
        far = lax.ppermute(keyvals, "seq", [(0, 1)])
    else:
        far = lax.all_gather(keyvals, "seq", axis=0, tiled=True)
    queries = (dot_nn(h_one, w_q) + b_qkv[:width]).astype(bf16)
    context, logsum = attend(limit, queries, keyvals, far)
    resid = hidden + dot_nn(context, w_out) + b_out

    normed_two, pull_two = jax.vjp(standardize_features, resid, gain_two, shift_two)
    h_two = normed_two.astype(bf16)
    upact = dot_nn(h_two, w_up) + b_up
    activ, gelu_pull = jax.vjp(gelu_apply, upact)
    act_low = activ.astype(bf16)
    out_delta = result_cotangent.reshape(tokens, width)
    down_part = dot_tn(act_low, out_delta).astype(bf16)
    down_part, act_low, out_delta = lax.optimization_barrier((down_part, act_low, out_delta))
    down_owned = lax.psum_scatter(down_part, "dp", scatter_dimension=0, tiled=True)
    out_float = out_delta.astype(f32)
    downshift_grad = jnp.sum(out_float, 0)
    up_delta = gelu_pull(dot_nt(out_delta, w_down))[0].astype(bf16)
    upshift_grad = jnp.sum(up_delta.astype(f32), 0)
    up_part = dot_tn(h_two, up_delta).astype(bf16)
    up_part, up_delta = lax.optimization_barrier((up_part, up_delta))
    up_owned = lax.psum_scatter(up_part, "dp", scatter_dimension=0, tiled=True)
    output = resid + dot_nn(act_low, w_down) + b_down
    norm_two_delta = dot_nt(up_delta, w_up)
    resid_part, midgain_grad, midshift_grad = pull_two(norm_two_delta)
    resid_grad = out_float + resid_part
    proj_delta = resid_grad.astype(bf16)
    outshift_grad = jnp.sum(proj_delta.astype(f32), 0)
    ctx_delta = dot_nt(proj_delta, w_out).astype(bf16)
    dq_far, dk_far, dv_far = attend_back_far(limit, queries, ctx_delta, context, logsum, far)
    if ranks == 2:
        dk_back = lax.ppermute(dk_far, "seq", [(1, 0)])
        dv_back = lax.ppermute(dv_far, "seq", [(1, 0)])
    else:
        dk_back = lax.psum_scatter(dk_far, "seq", scatter_dimension=0, tiled=True)
        dv_back = lax.psum_scatter(dv_far, "seq", scatter_dimension=0, tiled=True)
    dq, dk_own, dv_own = attend_back_own(queries, ctx_delta, context, logsum, keyvals, dq_far)
    out_part = dot_tn(context, proj_delta).astype(bf16)
    qkv_delta = jnp.concatenate(
        [
            dq,
            (dk_own + dk_back.astype(f32)).astype(bf16),
            (dv_own + dv_back.astype(f32)).astype(bf16),
        ],
        1,
    )
    qkvshift_grad = jnp.sum(qkv_delta.astype(f32), 0)
    qkv_part = dot_tn(h_one, qkv_delta).astype(bf16)
    input_portion, prenorm_gain_gradient, prenorm_shift_gradient = pull_one(
        dot_nt(qkv_delta, w_qkv)
    )
    input_grad = resid_grad + input_portion
    small_parts = (
        prenorm_gain_gradient,
        prenorm_shift_gradient,
        qkvshift_grad,
        outshift_grad,
        midgain_grad,
        midshift_grad,
        upshift_grad,
        downshift_grad,
    )
    small_part = pack_rows(
        [part.astype(bf16).reshape(shards, -1) for part in small_parts], rows
    )
    attn_owned = lax.psum_scatter(
        jnp.concatenate([qkv_part, out_part, small_part], 1),
        "dp",
        scatter_dimension=0,
        tiled=True,
    )
    upmatrix_grad = swap_sum(up_owned, ranks)
    downmatrix_grad = swap_sum(down_owned, ranks)
    attn_sum = swap_sum(attn_owned, ranks)
    gain_g, shift_g, qkvshift, outshift, midgain, midshift, upshift, downshift = unpack_rows(
        attn_sum[:, 4 * width :], 1, lengths
    )
    return (
        output.reshape(1, tokens, width),
        input_grad.reshape(1, tokens, width),
        gain_g,
        shift_g,
        attn_sum[:, : 3 * width],
        qkvshift,
        attn_sum[:, 3 * width : 4 * width],
        outshift,
        midgain,
        midshift,
        upmatrix_grad,
        upshift,
        downmatrix_grad,
        downshift,
    )


def solution(mesh):
    in_specs = (
        P("dp", "seq", None),
        P("dp", "seq", None),
        P("dp"),
        P("dp"),
        P("dp", None),
        P("dp"),
        P("dp", None),
        P("dp"),
        P("dp"),
        P("dp"),
        P("dp", None),
        P("dp"),
        P("dp", None),
        P("dp"),
    )
    out_specs = (
        P("dp", "seq", None),
        P("dp", "seq", None),
        P("dp"),
        P("dp"),
        P("dp", None),
        P("dp"),
        P("dp", None),
        P("dp"),
        P("dp"),
        P("dp"),
        P("dp", None),
        P("dp"),
        P("dp", None),
        P("dp"),
    )
    body = functools.partial(local, shards=mesh.shape["dp"], ranks=mesh.shape["seq"])
    return jax.shard_map(body, mesh=mesh, in_specs=in_specs, out_specs=out_specs, check_vma=False)
```

time: 895 us -> 615 us (0.69)
  blocking collectives: 198 us -> 0 us
  matrix products: 239 us -> 93.6 us
  waiting for transfers between devices: 325 us -> 387 us
  Pallas kernels: 0 us -> 60.6 us
  local copies, waits for them, and re-layouts: 50.6 us -> 22.3 us
  other arithmetic: 38.9 us -> 22.1 us
    dot_general x108 -> x13, matrix products: 239 us -> 93.6 us  [the longest x5 37 us: dot_nn(): return jnp.dot(left, right, preferred_element_type=jnp.float32)]
    unnamed x2 -> x0, blocking collectives: 124 us -> none
    all_gather x3 -> x2, waiting for transfers between devices: 0.04 us -> 77.2 us  [the longest x1 77.2 us: local(): lax.all_gather(jnp.concatenate([query_key_value_matrix, attention_exit_ma...]
    ppermute x0 -> x6, waiting for transfers between devices: none -> 69.1 us  [the longest x1 40.6 us: local(): far = lax.ppermute(keyvals, 'seq', [(0, 1)])]
    pallas_call x0 -> x3, Pallas kernels: none -> 60.6 us  [the longest x1 21.9 us: attend(): pl.pallas_call(forward_kernel, grid=(pairs,), in_specs=[LIMIT_SPEC, pair_...]
    all_to_all x1 -> x0, blocking collectives: 51.4 us -> none  [local(): lax.all_to_all(qkv_heads_delta, 'seq', split_axis=0, concat_axis=2, tiled...]
    all_to_all x3 -> x0, waiting for transfers between devices: 44.3 us -> none  [the longest x1 25.4 us: local(): lax.all_to_all(qkv_low, 'seq', split_axis=2, concat_axis=0, tiled=True)]
    psum x1 -> x0, waiting for transfers between devices: 41.1 us -> none  [local(): lax.psum(owned[2].astype(jnp.bfloat16), 'seq').astype(jnp.float32)]
  transfers between devices with their start and end apart: 12 -> 12, of which waited for: 7 -> 7; matrix products, arithmetic and copies ran while one was open for 32% -> 16% of each run, Pallas kernels for 0% -> 10%
where the time goes in v1:
time: 615 us; the launch traced here: 611 us
  waiting for transfers between devices  387 us (63%)
  matrix products  93.6 us (15%)
  Pallas kernels  60.6 us (10%)
  local copies, waits for them, and re-layouts  22.3 us (4%)
  other arithmetic  22.1 us (4%)
  between operations  14.8 us (2%)
  starting transfers between devices  11.3 us (2%)
    reduce_scatter x1, waiting for transfers between devices, local(): lax.psum_scatter(jnp.concatenate([qkv_part, out_part, small_part], 1), 'd...  109 us
    reduce_scatter x1, waiting for transfers between devices, local(): lax.psum_scatter(down_part, 'dp', scatter_dimension=0, tiled=True)  82.5 us
    all_gather x1, waiting for transfers between devices, local(): lax.all_gather(jnp.concatenate([query_key_value_matrix, attention_exit_ma...  77.2 us
    all_gather x1, waiting for transfers between devices, local(): lax.all_gather(contract_projection_matrix, 'dp', axis=0, tiled=True)  46.5 us
    ppermute x1, waiting for transfers between devices, local(): far = lax.ppermute(keyvals, 'seq', [(0, 1)])  40.6 us
    dot_general x5, matrix products, dot_nn(): return jnp.dot(left, right, preferred_element_type=jnp.float32)  37 us
    dot_general x4, matrix products, dot_nt(): lax.dot_general(left, right, (((1,), (1,)), ((), ())), preferred_element_...  34.9 us
    pallas_call x1, Pallas kernels, attend(): pl.pallas_call(forward_kernel, grid=(pairs,), in_specs=[LIMIT_SPEC, pair_...  21.9 us
  transfers between devices with their start and end apart: 12, of which 7 were waited for; matrix products, arithmetic and copies ran while one was open for 16% of the time, Pallas kernels for 10%

profile of v1, /device:TPU:0, one launch (start us, length us, event | category | flops | bytes accessed | tf_op | source)
XLA Modules:
  0.0 611.4 jit_solution(13935747956686727463)
XLA Ops:
  7.2 0.7 broadcast_in_dim.51
  8.0 0.7 broadcast_in_dim.55
  8.6 0.8 concatenate.15
  9.5 1.9 pad_maximum_fusion.2
  11.5 0.7 all-gather.6.cloned.1.call-update
  12.2 0.7 all-gather.8.cloned.1.call-update
  13.2 0.4 fusion.24
  13.6 77.2 %all-gather.4.cloned.1.call-done = bf16[1024,4224]{1,0:T(8,128)(2,1)} async-done(((bf16[64,4224]{1,0:T(8,128)(2,1)}), bf16[1024,4224]{1,0:T(8,128)(2,1)}) %all-gather.4.cloned.1.call-update) | async-done | bytes 8650768 | tf_op jit(solution)/shard_map/all_gather | solution.py:295
  90.8 1.0 slice.104
  92.2 4.6 add_convert_fusion.k_ref.v_ref
  96.9 4.9 collective-permute-start
  102.0 2.9 add_convert_fusion.4.q_ref
  104.9 40.6 %collective-permute-done.kr_ref.vr_ref = bf16[512,2048]{1,0:T(8,128)(2,1)} collective-permute-done((bf16[512,2048]{1,0:T(8,128)(2,1)S(1)}, bf16[512,2048]{1,0:T(8,128)(2,1)}, u32[]{:S(2)}, u32[]{:S(2)}) %collective-permute-start) | collective-permute-done | bytes 2097184 | tf_op jit(solution)/shard_map/ppermute | solution.py:315
  145.6 21.9 %attend.1 = (bf16[512,1024]{1,0:T(8,128)(2,1)S(1)}, f32[512,1024]{1,0:T(8,128)S(1)}) custom-call(s32[1]{0:T(128)} %bitcast.1.limit_ref, bf16[512,1024]{1,0:T(8,128)(2,1)S(1)} %add_convert_fusion.4.q_ref, bf16[512,2048]{1,0:T(8,128)(2,1)S(1)} %add_convert_fusion.k_ref.v_ref, bf16[512,2048]{1,0:T(8,128)(2,1)S(1)} %add_convert_fusion.k_ref.v_ref, ...), custom_call_target="tpu_custom_call" | custom-call | flops 8589934592 | bytes 12582912 | tf_op jit(solution)/shard_map/attend/pallas_call | solution.py:172
  167.5 4.1 fusion.56
  171.6 1.3 copy-done.17
  173.3 13.0 %multiply_convert_fusion = (bf16[512,4096]{1,0:T(8,128)(2,1)S(1)}, f32[512,4096]{1,0:T(8,128)}) fusion(f32[4096]{0:T(1024)S(1)} %bitcast.92, bf16[1024,4096]{1,0:T(8,128)(2,1)} %all-gather.6.cloned.1.call-done, f32[512,1024]{1,0:T(8,128)} %copy-done.17, f32[1024]{0:T(1024)S(1)} %reshape.248, f32[1024]{0:T(1024)S(1)} %reshape.247, f32[512]{0:T(512)S(1)} %fusion.42, ...), kind=kOutput, calls=%fused_computation.10 | convolution fusion | flops 4318560256 | bytes 23097344 | tf_op jit(solution)/shard_map/dot_general | solution.py:41
  186.3 1.9 copy-done.26
  188.2 6.7 %convolution_convert_fusion.1 = bf16[4096,1024]{1,0:T(8,128)(2,1)} fusion(bf16[512,4096]{1,0:T(8,128)(2,1)S(1)} %get-tuple-element.28, bf16[1,512,1024]{2,1,0:T(8,128)(2,1)S(1)} %copy-done.20), kind=kOutput, calls=%fused_computation.12 | convolution fusion | flops 4299161600 | bytes 13631488 | tf_op jit(solution)/shard_map/dot_general | solution.py:35
  194.9 46.5 %all-gather.8.cloned.1.call-done = bf16[4096,1024]{1,0:T(8,128)(2,1)} async-done(((bf16[256,1024]{1,0:T(8,128)(2,1)}), bf16[4096,1024]{1,0:T(8,128)(2,1)}) %all-gather.8.cloned.1.call-update) | async-done | bytes 8388624 | tf_op jit(solution)/shard_map/all_gather | solution.py:302
  241.5 13.7 %fusion.51 = (bf16[4096]{0:T(1024)(128)(2,1)S(1)}, bf16[512,4096]{1,0:T(8,128)(2,1)S(1)}) fusion(f32[512,4096]{1,0:T(8,128)} %get-tuple-element.69, f32[4096]{0:T(1024)S(1)} %bitcast.93, bf16[512,1024]{1,0:T(8,128)(2,1)} %bitcast.85, bf16[4096,1024]{1,0:T(8,128)(2,1)} %all-gather.8.cloned.1.call-done), kind=kOutput, calls=%fused_computation.91 | convolution fusion | flops 4341100544 | bytes 22044672 | tf_op jit(solution)/shard_map/dot_general | solution.py:29
  255.1 1.9 copy-done.27
  257.1 7.2 %convolution_convert_fusion = bf16[1024,4096]{1,0:T(8,128)(2,1)} fusion(bf16[512,4096]{1,0:T(8,128)(2,1)S(1)} %get-tuple-element.30, f32[512,1024]{1,0:T(8,128)S(1)} %copy-done.18, f32[1024]{0:T(1024)S(1)} %reshape.248, f32[1024]{0:T(1024)S(1)} %reshape.247, f32[512]{0:T(512)S(1)} %fusion.42, f32[512]{0:T(512)S(1)} %broadcast_multiply_fusion), kind=kOutput, calls=%fused_computation.11 | convolution fusion | flops 4301783040 | bytes 14692352 | tf_op jit(solution)/shard_map/dot_general | solution.py:35
  264.4 0.5 reduce-scatter.8.cloned.1.call-update
  264.9 0.5 reduce-scatter.4.cloned.1.call-start
  265.4 11.1 %multiply_reduce_fusion = (bf16[1024]{0:T(1024)(128)(2,1)S(1)}, f32[512]{0:T(512)S(1)}, bf16[1024]{0:T(1024)(128)(2,1)S(1)}, f32[512,1024]{1,0:T(8,128)S(1)}) fusion(f32[512,1024]{1,0:T(8,128)} %copy-done.17, f32[512]{0:T(512)S(1)} %fusion.42, f32[512]{0:T(512)S(1)} %broadcast_multiply_fusion, f32[1024]{0:T(1024)S(1)} %reshape.247, ...), kind=kOutput, calls=%fused_computation.40 | convolution fusion | flops 4299159040 | bytes 16791552 | tf_op jit(solution)/shard_map/dot_general | solution.py:29
  276.6 0.7 fusion.55
  277.3 0.6 copy-done.21
  277.9 0.6 fusion.53
  278.6 3.3 fusion.35.g_ref
  281.9 20.6 %attend_back_far.1 = (f32[512,1024]{1,0:T(8,128)S(1)}, bf16[512,1024]{1,0:T(8,128)(2,1)}, bf16[512,1024]{1,0:T(8,128)(2,1)}) custom-call(s32[1]{0:T(128)} %bitcast.1.limit_ref, bf16[512,1024]{1,0:T(8,128)(2,1)S(1)} %copy-done.5, bf16[512,1024]{1,0:T(8,128)(2,1)S(1)} %fusion.35.g_ref, bf16[512,1024]{1,0:T(8,128)(2,1)S(1)} %get-tuple-element.27.ctx_ref, ...), custom_call_target="tpu_custom_call" | custom-call | flops 10737418240 | bytes 8388608 | tf_op jit(solution)/shard_map/attend_back_far/pallas_call | solution.py:198
  302.6 1.3 collective-permute-start.2
  303.9 2.7 convolution_convert_fusion.3
  306.6 1.5 collective-permute-start.1
  308.3 1.2 copy-done.1
  309.6 1.2 copy-done.3
  310.8 1.2 copy-done.6
  312.0 1.7 copy-done.9
  313.7 18.1 %attend_back_own.1 = (bf16[512,1024]{1,0:T(8,128)(2,1)S(1)}, f32[512,1024]{1,0:T(8,128)S(1)}, f32[512,1024]{1,0:T(8,128)S(1)}) custom-call(bf16[512,1024]{1,0:T(8,128)(2,1)S(1)} %copy-done.6, bf16[512,1024]{1,0:T(8,128)(2,1)S(1)} %copy-done.3, bf16[512,1024]{1,0:T(8,128)(2,1)S(1)} %copy-done.1, f32[512,1024]{1,0:T(8,128)S(1)} %copy-done.9, ...), custom_call_target="tpu_custom_call" | custom-call | flops 10737418240 | bytes 8388608 | tf_op jit(solution)/shard_map/attend_back_own/pallas_call | solution.py:219
  331.8 1.6 add_convert_fusion.1
  333.4 19.1 %collective-permute-done.1 = bf16[512,1024]{1,0:T(8,128)(2,1)} collective-permute-done((bf16[512,1024]{1,0:T(8,128)(2,1)}, bf16[512,1024]{1,0:T(8,128)(2,1)}, u32[]{:S(2)}, u32[]{:S(2)}) %collective-permute-start.1) | collective-permute-done | bytes 1048608 | tf_op jit(solution)/shard_map/ppermute | solution.py:347
  352.6 1.7 add_convert_fusion.2
  354.3 6.9 %fusion.50 = (bf16[1024]{0:T(1024)(128)(2,1)S(1)}, f32[512]{0:T(512)S(1)}, f32[512,1024]{1,0:T(8,128)S(1)}) fusion(f32[1024]{0:T(1024)S(1)} %reshape.243, f32[512]{0:T(512)S(1)} %broadcast_multiply_fusion.1, bf16[1,512,1024]{2,1,0:T(8,128)(2,1)S(1)} %copy-done.15, bf16[1024,4224]{1,0:T(8,128)(2,1)} %all-gather.4.cloned.1.call-done, ...), kind=kOutput, calls=%fused_computation.90 | convolution fusion | flops 3233806848 | bytes 12593152 | tf_op jit(solution)/shard_map/dot_general | solution.py:29
  361.2 1.3 copy-done.16
  362.5 1.0 fusion.23
  363.6 1.6 fusion.44
  365.4 0.7 pad.9
  366.1 1.1 reshape.233
  367.2 5.0 convolution_convert_fusion.2
  372.3 3.9 pad_maximum_fusion
  376.3 12.3 %add_bitcast_fusion.1 = f32[1,512,1024]{2,1,0:T(8,128)} fusion(f32[512,1024]{1,0:T(8,128)} %copy-done.17, bf16[512,4096]{1,0:T(8,128)(2,1)} %copy-done.26, bf16[4096,1024]{1,0:T(8,128)(2,1)} %all-gather.8.cloned.1.call-done, f32[1024]{0:T(1024)S(1)} %reshape.250), kind=kOutput, calls=%fused_computation.46 | convolution fusion | flops 4296015872 | bytes 16781312 | tf_op jit(solution)/shard_map/dot_general | solution.py:41
  388.7 4.5 add_bitcast_fusion
  393.1 82.5 %reduce-scatter.8.cloned.1.call-done = bf16[256,1024]{1,0:T(8,128)(2,1)} async-done(((bf16[4096,1024]{1,0:T(8,128)(2,1)}), bf16[256,1024]{1,0:T(8,128)(2,1)}) %reduce-scatter.8.cloned.1.call-update) | async-done | bytes 524304 | tf_op jit(solution)/shard_map/reduce_scatter | solution.py:330
  475.6 1.5 collective-permute-start.5
  477.1 109.4 %reduce-scatter.4.cloned.1.call-done = bf16[64,4224]{1,0:T(8,128)(2,1)} async-done(((bf16[1024,4224]{1,0:T(8,128)(2,1)}), bf16[64,4224]{1,0:T(8,128)(2,1)}) %reduce-scatter.4.cloned.1.call-update) | async-done | bytes 540688 | tf_op jit(solution)/shard_map/reduce_scatter | solution.py:381
  586.5 1.5 collective-permute-start.3
  588.0 2.3 convert_add_fusion.2
  590.3 1.1 convert_add_fusion.1
  591.4 9.3 %collective-permute-done.3 = bf16[64,4224]{1,0:T(8,128)(2,1)S(1)} collective-permute-done((bf16[64,4224]{1,0:T(8,128)(2,1)}, bf16[64,4224]{1,0:T(8,128)(2,1)S(1)}, u32[]{:S(2)}, u32[]{:S(2)}) %collective-permute-start.3) | collective-permute-done | bytes 540704 | tf_op jit(solution)/shard_map/ppermute | solution.py:254
  600.9 0.9 slice.122
  601.8 0.6 slice_bitcast_fusion
  602.4 0.6 slice.123
  603.0 0.7 slice.124
  603.7 0.6 slice.128
  (97 shorter events, 2.6 us)
Async XLA Ops:
  7.2 5.8 copy-start.13
  7.2 83.6 %all-gather.4.cloned.1.call-start = ((), (), s32[]{:S(2)}) async-start(), calls=%async_computation.3 | async-start | bytes 9191424 | tf_op jit(solution)/shard_map/all_gather | solution.py:295
  11.4 161.8 %all-gather.6.cloned.1.call-start = ((), (), s32[]{:S(2)}) async-start(), calls=%async_computation.4 | async-start | bytes 8912896 | tf_op jit(solution)/shard_map/all_gather | solution.py:301
  12.2 229.3 %all-gather.8.cloned.1.call-start = ((), (), s32[]{:S(2)}) async-start(), calls=%async_computation.5 | async-start | bytes 8912896 | tf_op jit(solution)/shard_map/all_gather | solution.py:302
  12.9 375.7 %reduce-scatter.6.cloned.1.call-start = ((), (), s32[]{:S(2)}) async-start(), calls=%async_computation.7 | async-start | bytes 8912896 | tf_op jit(solution)/shard_map/reduce_scatter | solution.py:337
  96.9 48.7 %collective-permute-start = (bf16[512,2048]{1,0:T(8,128)(2,1)S(1)}, bf16[512,2048]{1,0:T(8,128)(2,1)}, u32[]{:S(2)}, u32[]{:S(2)}) collective-permute-start(bf16[512,2048]{1,0:T(8,128)(2,1)S(1)} %add_convert_fusion.k_ref.v_ref), channel_id=1, source_target_pairs={{0,1},{2,3},{4,5},{6,7},{8,9},{10,11},{12,13},{14,15},{16,17},{18,... | collective-permute-start | bytes 6291464 | tf_op jit(solution)/shard_map/ppermute | solution.py:315
  104.9 62.5 %copy-start.4 = (bf16[512,1024]{1,0:T(8,128)(2,1)}, bf16[512,1024]{1,0:T(8,128)(2,1)S(1)}, u32[]{:S(2)}) copy-start(bf16[512,1024]{1,0:T(8,128)(2,1)S(1)} %add_convert_fusion.4.q_ref) | copy-start | bytes 3145732
  145.6 21.9 %copy-start.14 = (bf16[1,512,1024]{2,1,0:T(8,128)(2,1)S(1)}, bf16[1,512,1024]{2,1,0:T(8,128)(2,1)}, u32[]{:S(2)}) copy-start(bf16[1,512,1024]{2,1,0:T(8,128)(2,1)} %param.14) | copy-start | bytes 3145732
  167.4 4.1 copy-start.7
  167.5 136.4 %copy-start = (bf16[512,1024]{1,0:T(8,128)(2,1)}, bf16[512,1024]{1,0:T(8,128)(2,1)S(1)}, u32[]{:S(2)}) copy-start(bf16[512,1024]{1,0:T(8,128)(2,1)S(1)} %get-tuple-element.27.ctx_ref) | copy-start | bytes 3145732
  171.6 1.3 copy-start.17
  173.3 15.0 %copy-start.20 = (bf16[1,512,1024]{2,1,0:T(8,128)(2,1)S(1)}, bf16[1,512,1024]{2,1,0:T(8,128)(2,1)}, u32[]{:S(2)}) copy-start(bf16[1,512,1024]{2,1,0:T(8,128)(2,1)} %param.15) | copy-start | bytes 3145732
  186.3 1.9 copy-start.26
  241.5 15.6 %copy-start.18 = (f32[512,1024]{1,0:T(8,128)S(1)}, f32[512,1024]{1,0:T(8,128)}, u32[]{:S(2)}) copy-start(f32[512,1024]{1,0:T(8,128)} %copy-done.17) | copy-start | bytes 6291460
  255.1 1.9 copy-start.27
  264.3 211.3 %reduce-scatter.8.cloned.1.call-start = ((), (), s32[]{:S(2)}) async-start(), calls=%async_computation.8 | async-start | bytes 8912896 | tf_op jit(solution)/shard_map/reduce_scatter | solution.py:330
  264.9 321.6 %reduce-scatter.4.cloned.1.call-start = ((), (), s32[]{:S(2)}) async-start(), calls=%async_computation.6 | async-start | bytes 9191424 | tf_op jit(solution)/shard_map/reduce_scatter | solution.py:381
  265.4 11.1 %copy-start.19 = (f32[512,1024]{1,0:T(8,128)S(1)}, f32[512,1024]{1,0:T(8,128)}, u32[]{:S(2)}) copy-start(f32[512,1024]{1,0:T(8,128)} %copy-done.17) | copy-start | bytes 6291460
  276.5 1.3 copy-start.21
  277.3 1.3 copy-start.11
  278.6 3.3 copy-start.5
  278.6 3.3 copy-start.8
  281.9 20.7 %copy-start.2 = (bf16[512,1024]{1,0:T(8,128)(2,1)}, bf16[512,1024]{1,0:T(8,128)(2,1)S(1)}, u32[]{:S(2)}) copy-start(bf16[512,1024]{1,0:T(8,128)(2,1)S(1)} %fusion.35.g_ref) | copy-start | bytes 3145732
  302.6 4.0 copy-start.10
  302.6 29.2 %collective-permute-start.2 = (bf16[512,1024]{1,0:T(8,128)(2,1)}, bf16[512,1024]{1,0:T(8,128)(2,1)}, u32[]{:S(2)}, u32[]{:S(2)}) collective-permute-start(bf16[512,1024]{1,0:T(8,128)(2,1)} %get-tuple-element.37), channel_id=1, source_target_pairs={{1,0},{3,2},{5,4},{7,6},{9,8},{11,10},{13,12},{15,14},{17,16},{19,... | collective-permute-start | bytes 3145736 | tf_op jit(solution)/shard_map/ppermute | solution.py:348
  306.6 46.0 %collective-permute-start.1 = (bf16[512,1024]{1,0:T(8,128)(2,1)}, bf16[512,1024]{1,0:T(8,128)(2,1)}, u32[]{:S(2)}, u32[]{:S(2)}) collective-permute-start(bf16[512,1024]{1,0:T(8,128)(2,1)} %get-tuple-element.35), channel_id=1, source_target_pairs={{1,0},{3,2},{5,4},{7,6},{9,8},{11,10},{13,12},{15,14},{17,16},{19,... | collective-permute-start | bytes 3145736 | tf_op jit(solution)/shard_map/ppermute | solution.py:347
  308.3 1.2 copy-start.1
  309.6 1.2 copy-start.3
  310.8 1.2 copy-start.6
  312.0 1.7 copy-start.9
  352.6 1.7 copy-start.15
  354.2 6.9 %copy-start.22 = (bf16[512,1024]{1,0:T(8,128)(2,1)}, bf16[512,1024]{1,0:T(8,128)(2,1)S(1)}, u32[]{:S(2)}) copy-start(bf16[512,1024]{1,0:T(8,128)(2,1)S(1)} %add_convert_fusion.2) | copy-start | bytes 3145732
  361.2 1.3 copy-start.16
  367.2 5.1 copy-start.23
  376.3 12.4 %copy-start.12 = (f32[512,1024]{1,0:T(8,128)S(1)}, f32[512,1024]{1,0:T(8,128)}, u32[]{:S(2)}) copy-start(f32[512,1024]{1,0:T(8,128)} %copy-done.11) | copy-start | bytes 6291460
  388.6 199.4 %collective-permute-start.4 = (bf16[64,4096]{1,0:T(8,128)(2,1)}, bf16[64,4096]{1,0:T(8,128)(2,1)}, u32[]{:S(2)}, u32[]{:S(2)}) collective-permute-start(bf16[64,4096]{1,0:T(8,128)(2,1)} %reduce-scatter.6.cloned.1.call-done), channel_id=1, source_target_pairs={{0,1},{1,0},{2,3},{3,2},{4,5},{5,4},{6,7},{7,6},{8,9},{9,8},{10,11... | collective-permute-start | bytes 1572872 | tf_op jit(solution)/shard_map/ppermute | solution.py:254
  475.6 114.7 %copy-start.25 = (bf16[256,1024]{1,0:T(8,128)(2,1)S(1)}, bf16[256,1024]{1,0:T(8,128)(2,1)}, u32[]{:S(2)}) copy-start(bf16[256,1024]{1,0:T(8,128)(2,1)} %reduce-scatter.8.cloned.1.call-done) | copy-start | bytes 1572868
  475.6 114.7 %collective-permute-start.5 = (bf16[256,1024]{1,0:T(8,128)(2,1)}, bf16[256,1024]{1,0:T(8,128)(2,1)S(1)}, u32[]{:S(2)}, u32[]{:S(2)}) collective-permute-start(bf16[256,1024]{1,0:T(8,128)(2,1)} %reduce-scatter.8.cloned.1.call-done), channel_id=1, source_target_pairs={{0,1},{1,0},{2,3},{3,2},{4,5},{5,4},{6,7},{7,6},{8,9},{9,8},{10,11... | collective-permute-start | bytes 1572872 | tf_op jit(solution)/shard_map/ppermute | solution.py:254
  586.5 14.3 %copy-start.24 = (bf16[64,4224]{1,0:T(8,128)(2,1)S(1)}, bf16[64,4224]{1,0:T(8,128)(2,1)}, u32[]{:S(2)}) copy-start(bf16[64,4224]{1,0:T(8,128)(2,1)} %reduce-scatter.4.cloned.1.call-done) | copy-start | bytes 1622020
  586.5 14.3 %collective-permute-start.3 = (bf16[64,4224]{1,0:T(8,128)(2,1)}, bf16[64,4224]{1,0:T(8,128)(2,1)S(1)}, u32[]{:S(2)}, u32[]{:S(2)}) collective-permute-start(bf16[64,4224]{1,0:T(8,128)(2,1)} %reduce-scatter.4.cloned.1.call-done), channel_id=1, source_target_pairs={{0,1},{1,0},{2,3},{3,2},{4,5},{5,4},{6,7},{7,6},{8,9},{9,8},{10,11... | collective-permute-start | bytes 1622024 | tf_op jit(solution)/shard_map/ppermute | solution.py:254
Sparse Core Ops, SparseCore 0:
  11.6 79.2 all-gather.3
  93.0 73.0 all-gather.5
  168.3 73.1 all-gather.7
  264.4 102.8 reduce-scatter.5
  371.2 104.3 reduce-scatter.7
  479.5 106.9 reduce-scatter.3

commit v2 on v1

--- a/solution.py
+++ b/solution.py
@@ -249,11 +249,50 @@
     return pieces
 
 
-def swap_sum(value, ranks):
-    if ranks == 2:
-        other = lax.ppermute(value, "seq", [(0, 1), (1, 0)])
-        return value.astype(jnp.float32) + other.astype(jnp.float32)
-    return lax.psum(value, "seq").astype(jnp.float32)
+def pick(blocks, index):
+    return lax.dynamic_index_in_dim(blocks, index, 1, keepdims=False)
+
+
+def swap_half(blocks, axis, pairs, mine):
+    other = lax.ppermute(pick(blocks, 1 - mine), axis, pairs)
+    total = pick(blocks, mine).astype(jnp.float32) + other.astype(jnp.float32)
+    return total.astype(jnp.bfloat16)
+
+
+def sum_cores(part, shards):
+    blocks = part.reshape(shards // 2, 2, part.shape[0] // shards, part.shape[-1])
+    core = lax.rem(lax.axis_index("dp"), 2)
+    pairs = [(i, i + 1 - 2 * (i % 2)) for i in range(shards)]
+    return swap_half(blocks, "dp", pairs, core)
+
+
+def sum_ranks(held, ranks):
+    if ranks != 2:
+        return held
+    blocks = held.reshape(held.shape[0], 2, held.shape[1] // 2, held.shape[2])
+    return swap_half(blocks, "seq", [(0, 1), (1, 0)], lax.axis_index("seq"))
+
+
+def sum_chips(held, shards):
+    return lax.psum_scatter(
+        held.reshape(-1, held.shape[-1]),
+        "dp",
+        scatter_dimension=0,
+        axis_index_groups=[list(range(0, shards, 2)), list(range(1, shards, 2))],
+        tiled=True,
+    )
+
+
+def finish_sum(owned, ranks, seq_first):
+    if ranks != 2:
+        return lax.psum(owned, "seq").astype(jnp.float32)
+    other = lax.ppermute(owned, "seq", [(0, 1), (1, 0)])
+    if not seq_first:
+        return owned.astype(jnp.float32) + other.astype(jnp.float32)
+    first = lax.axis_index("seq") == 0
+    top = jnp.where(first, owned, other)
+    bottom = jnp.where(first, other, owned)
+    return jnp.concatenate([top, bottom], 0).astype(jnp.float32)
 
 
 def local(
@@ -326,15 +365,17 @@
     act_low = activ.astype(bf16)
     out_delta = result_cotangent.reshape(tokens, width)
     down_part = dot_tn(act_low, out_delta).astype(bf16)
-    down_part, act_low, out_delta = lax.optimization_barrier((down_part, act_low, out_delta))
-    down_owned = lax.psum_scatter(down_part, "dp", scatter_dimension=0, tiled=True)
+    down_held = sum_cores(down_part, shards)
+    down_held, act_low, out_delta = lax.optimization_barrier((down_held, act_low, out_delta))
+    down_held = sum_ranks(down_held, ranks)
     out_float = out_delta.astype(f32)
     downshift_grad = jnp.sum(out_float, 0)
     up_delta = gelu_pull(dot_nt(out_delta, w_down))[0].astype(bf16)
     upshift_grad = jnp.sum(up_delta.astype(f32), 0)
     up_part = dot_tn(h_two, up_delta).astype(bf16)
-    up_part, up_delta = lax.optimization_barrier((up_part, up_delta))
-    up_owned = lax.psum_scatter(up_part, "dp", scatter_dimension=0, tiled=True)
+    up_part, up_delta, down_held = lax.optimization_barrier((up_part, up_delta, down_held))
+    down_owned = sum_chips(down_held, shards)
+    up_held = sum_cores(up_part, shards)
     output = resid + dot_nn(act_low, w_down) + b_down
     norm_two_delta = dot_nt(up_delta, w_up)
     resid_part, midgain_grad, midshift_grad = pull_two(norm_two_delta)
@@ -349,8 +390,11 @@
     else:
         dk_back = lax.psum_scatter(dk_far, "seq", scatter_dimension=0, tiled=True)
         dv_back = lax.psum_scatter(dv_far, "seq", scatter_dimension=0, tiled=True)
+    up_held, dq_far = lax.optimization_barrier((up_held, dq_far))
+    up_owned = sum_chips(up_held, shards)
     dq, dk_own, dv_own = attend_back_own(queries, ctx_delta, context, logsum, keyvals, dq_far)
     out_part = dot_tn(context, proj_delta).astype(bf16)
+    down_owned, dq, dk_own, dv_own = lax.optimization_barrier((down_owned, dq, dk_own, dv_own))
     qkv_delta = jnp.concatenate(
         [
             dq,
@@ -378,15 +422,14 @@
     small_part = pack_rows(
         [part.astype(bf16).reshape(shards, -1) for part in small_parts], rows
     )
-    attn_owned = lax.psum_scatter(
-        jnp.concatenate([qkv_part, out_part, small_part], 1),
-        "dp",
-        scatter_dimension=0,
-        tiled=True,
-    )
-    upmatrix_grad = swap_sum(up_owned, ranks)
-    downmatrix_grad = swap_sum(down_owned, ranks)
-    attn_sum = swap_sum(attn_owned, ranks)
+    attn_held = sum_ranks(
+        sum_cores(jnp.concatenate([qkv_part, out_part, small_part], 1), shards), ranks
+    )
+    up_owned, attn_held = lax.optimization_barrier((up_owned, attn_held))
+    attn_owned = sum_chips(attn_held, shards)
+    upmatrix_grad = finish_sum(up_owned, ranks, False)
+    downmatrix_grad = finish_sum(down_owned, ranks, True)
+    attn_sum = finish_sum(attn_owned, ranks, True)
     gain_g, shift_g, qkvshift, outshift, midgain, midshift, upshift, downshift = unpack_rows(
         attn_sum[:, 4 * width :], 1, lengths
     )

time: 615 us -> 570 us (0.927)
  waiting for transfers between devices: 387 us -> 306 us
  other arithmetic: 22.1 us -> 44.5 us
  local copies, waits for them, and re-layouts: 22.3 us -> 31.6 us
    reduce_scatter x3, waiting for transfers between devices: 192 us -> 72.4 us  [sum_chips(): lax.psum_scatter(held.reshape(-1, held.shape[-1]), 'dp', scatter_dimensio...]
    ppermute x3 -> x8, waiting for transfers between devices: 9.35 us -> 73.7 us  [the longest x5 64 us: swap_half(): other = lax.ppermute(pick(blocks, 1 - mine), axis, pairs)]
    convert_element_type x0 -> x7, other arithmetic: none -> 24.7 us  [the longest x5 23.5 us: swap_half(): return total.astype(jnp.bfloat16)]
    all_gather x1, waiting for transfers between devices: 46.5 us -> 25.6 us  [local(): lax.all_gather(contract_projection_matrix, 'dp', axis=0, tiled=True)]
    ppermute x1, waiting for transfers between devices: 19.1 us -> 0.01 us  [local(): dk_back = lax.ppermute(dk_far, 'seq', [(1, 0)])]
    ppermute x1, waiting for transfers between devices: 0.01 us -> 14.9 us  [local(): dv_back = lax.ppermute(dv_far, 'seq', [(1, 0)])]
    squeeze x0 -> x5, local copies, waits for them, and re-layouts: none -> 11.9 us  [pick(): return lax.dynamic_index_in_dim(blocks, index, 1, keepdims=False)]
    unnamed x57 -> x75, local copies, waits for them, and re-layouts: 12.6 us -> 12.6 us
  transfers between devices with their start and end apart: 12 -> 17, of which waited for: 7 -> 11; matrix products, arithmetic and copies ran while one was open for 16% -> 20% of each run, Pallas kernels for 10% -> 11%
where the time goes in v2:
time: 570 us; the launch traced here: 565 us
  waiting for transfers between devices  306 us (54%)
  matrix products  93.2 us (16%)
  Pallas kernels  60.9 us (11%)
  other arithmetic  44.5 us (8%)
  local copies, waits for them, and re-layouts  31.6 us (6%)
  between operations  14.9 us (3%)
  starting transfers between devices  14.2 us (2%)
    all_gather x1, waiting for transfers between devices, local(): lax.all_gather(jnp.concatenate([query_key_value_matrix, attention_exit_ma...  77.2 us
    reduce_scatter x3, waiting for transfers between devices, sum_chips(): lax.psum_scatter(held.reshape(-1, held.shape[-1]), 'dp', scatter_dimensio...  72.4 us
    ppermute x5, waiting for transfers between devices, swap_half(): other = lax.ppermute(pick(blocks, 1 - mine), axis, pairs)  64 us
    ppermute x1, waiting for transfers between devices, local(): far = lax.ppermute(keyvals, 'seq', [(0, 1)])  40.7 us
    dot_general x5, matrix products, dot_nn(): return jnp.dot(left, right, preferred_element_type=jnp.float32)  35.8 us
    dot_general x4, matrix products, dot_nt(): lax.dot_general(left, right, (((1,), (1,)), ((), ())), preferred_element_...  34.3 us
    all_gather x1, waiting for transfers between devices, local(): lax.all_gather(contract_projection_matrix, 'dp', axis=0, tiled=True)  25.6 us
    convert_element_type x5, other arithmetic, swap_half(): return total.astype(jnp.bfloat16)  23.5 us
  transfers between devices with their start and end apart: 17, of which 11 were waited for; matrix products, arithmetic and copies ran while one was open for 20% of the time, Pallas kernels for 11%

profile of v2, /device:TPU:0, one launch (start us, length us, event | category | flops | bytes accessed | tf_op | source)
XLA Modules:
  0.0 565.3 jit_solution(13701908370219465923)
XLA Ops:
  7.2 0.7 broadcast_in_dim.51
  8.6 0.8 concatenate.28
  9.5 1.9 pad_maximum_fusion.2
  11.5 0.7 all-gather.6.cloned.1.call-update
  13.6 77.2 %all-gather.4.cloned.1.call-done = bf16[1024,4224]{1,0:T(8,128)(2,1)} async-done(((bf16[64,4224]{1,0:T(8,128)(2,1)}), bf16[1024,4224]{1,0:T(8,128)(2,1)}) %all-gather.4.cloned.1.call-update) | async-done | bytes 8650768 | tf_op jit(solution)/shard_map/all_gather | solution.py:334
  90.8 1.0 slice.104
  92.8 4.6 add_convert_fusion.k_ref.v_ref
  97.4 4.8 collective-permute-start
  102.4 2.9 add_convert_fusion.4.q_ref
  105.3 40.7 %collective-permute-done.kr_ref.vr_ref = bf16[512,2048]{1,0:T(8,128)(2,1)} collective-permute-done((bf16[512,2048]{1,0:T(8,128)(2,1)S(1)}, bf16[512,2048]{1,0:T(8,128)(2,1)}, u32[]{:S(2)}, u32[]{:S(2)}) %collective-permute-start) | collective-permute-done | bytes 2097184 | tf_op jit(solution)/shard_map/ppermute | solution.py:354
  146.1 22.0 %attend.1 = (bf16[512,1024]{1,0:T(8,128)(2,1)S(1)}, f32[512,1024]{1,0:T(8,128)S(1)}) custom-call(s32[1]{0:T(128)} %bitcast.1.limit_ref, bf16[512,1024]{1,0:T(8,128)(2,1)S(1)} %add_convert_fusion.4.q_ref, bf16[512,2048]{1,0:T(8,128)(2,1)S(1)} %add_convert_fusion.k_ref.v_ref, bf16[512,2048]{1,0:T(8,128)(2,1)S(1)} %add_convert_fusion.k_ref.v_ref, ...), custom_call_target="tpu_custom_call" | custom-call | flops 8589934592 | bytes 12582912 | tf_op jit(solution)/shard_map/attend/pallas_call | solution.py:172
  168.2 4.1 fusion.61
  172.7 13.0 %multiply_convert_fusion = (bf16[512,4096]{1,0:T(8,128)(2,1)S(1)}, f32[512,4096]{1,0:T(8,128)}) fusion(f32[4096]{0:T(1024)S(1)} %bitcast.146, bf16[1024,4096]{1,0:T(8,128)(2,1)} %all-gather.6.cloned.1.call-done, f32[512,1024]{1,0:T(8,128)S(1)} %get-tuple-element.89, f32[1024]{0:T(1024)S(1)} %reshape.288, f32[1024]{0:T(1024)S(1)} %reshape.287, ...), kind=kOutput, calls=%fused_computation.16 | convolution fusion | flops 4318560256 | bytes 23097344 | tf_op jit(solution)/shard_map/dot_general | solution.py:41
  185.7 4.8 convolution_convert_fusion.1
  190.5 3.2 copy-done.25
  193.8 2.8 dynamic-slice_bitcast_fusion.2
  196.6 7.5 %collective-permute-done.1 = bf16[8,256,1024]{2,1,0:T(8,128)(2,1)} collective-permute-done((bf16[8,256,1024]{2,1,0:T(8,128)(2,1)}, bf16[8,256,1024]{2,1,0:T(8,128)(2,1)}, u32[]{:S(2)}, u32[]{:S(2)}) %collective-permute-start.1) | collective-permute-done | bytes 4194336 | tf_op jit(solution)/shard_map/ppermute | solution.py:257
  204.1 5.6 fusion.9
  209.7 2.0 copy-done.17
  211.7 1.5 dynamic-slice_bitcast_fusion.4
  213.3 2.5 collective-permute-start.2
  215.8 25.6 %all-gather.8.cloned.1.call-done = bf16[4096,1024]{1,0:T(8,128)(2,1)} async-done(((bf16[256,1024]{1,0:T(8,128)(2,1)}), bf16[4096,1024]{1,0:T(8,128)(2,1)}) %all-gather.8.cloned.1.call-update) | async-done | bytes 8388624 | tf_op jit(solution)/shard_map/all_gather | solution.py:341
  241.5 15.0 %fusion.56 = (bf16[4096]{0:T(1024)(128)(2,1)S(1)}, bf16[512,4096]{1,0:T(8,128)(2,1)}) fusion(f32[512,4096]{1,0:T(8,128)} %get-tuple-element.91, f32[4096]{0:T(1024)S(1)} %bitcast.147, bf16[512,1024]{1,0:T(8,128)(2,1)} %bitcast.137, bf16[4096,1024]{1,0:T(8,128)(2,1)} %all-gather.8.cloned.1.call-done), kind=kOutput, calls=%fused_computation.113 | convolution fusion | flops 4341100544 | bytes 22044672 | tf_op jit(solution)/shard_map/dot_general | solution.py:29
  256.5 9.3 %convolution_convert_fusion = bf16[1024,4096]{1,0:T(8,128)(2,1)} fusion(bf16[512,4096]{1,0:T(8,128)(2,1)} %get-tuple-element.40, f32[512,1024]{1,0:T(8,128)S(1)} %get-tuple-element.89, f32[1024]{0:T(1024)S(1)} %reshape.288, f32[1024]{0:T(1024)S(1)} %reshape.287, f32[512]{0:T(512)S(1)} %fusion.47, f32[512]{0:T(512)S(1)} %broadcast_multiply_fusion), kind=kOutput, calls=%fused_computation.17 | convolution fusion | flops 4301783040 | bytes 14692352 | tf_op jit(solution)/shard_map/dot_general | solution.py:35
  265.8 3.9 fusion.15
  269.7 4.7 dynamic-slice_bitcast_fusion.1
  274.7 9.2 %multiply_reduce_fusion = (bf16[1024]{0:T(1024)(128)(2,1)S(1)}, f32[512]{0:T(512)S(1)}, bf16[1024]{0:T(1024)(128)(2,1)S(1)}, f32[512,1024]{1,0:T(8,128)S(1)}) fusion(f32[512,1024]{1,0:T(8,128)S(1)} %get-tuple-element.89, f32[512]{0:T(512)S(1)} %fusion.47, f32[512]{0:T(512)S(1)} %broadcast_multiply_fusion, f32[1024]{0:T(1024)S(1)} %reshape.287, ...), kind=kOutput, calls=%fused_computation.54 | convolution fusion | flops 4299159040 | bytes 16791552 | tf_op jit(solution)/shard_map/dot_general | solution.py:29
  284.0 0.7 fusion.60
  285.8 3.0 fusion.40.g_ref
  288.9 20.6 %attend_back_far.1 = (f32[512,1024]{1,0:T(8,128)S(1)}, bf16[512,1024]{1,0:T(8,128)(2,1)}, bf16[512,1024]{1,0:T(8,128)(2,1)}) custom-call(s32[1]{0:T(128)} %bitcast.1.limit_ref, bf16[512,1024]{1,0:T(8,128)(2,1)S(1)} %copy-done.8, bf16[512,1024]{1,0:T(8,128)(2,1)S(1)} %fusion.40.g_ref, bf16[512,1024]{1,0:T(8,128)(2,1)S(1)} %get-tuple-element.36.ctx_ref, ...), custom_call_target="tpu_custom_call" | custom-call | flops 10737418240 | bytes 8388608 | tf_op jit(solution)/shard_map/attend_back_far/pallas_call | solution.py:198
  309.4 1.4 copy-done.13
  310.8 1.3 collective-permute-start.4
  312.1 1.3 collective-permute-start.5
  313.7 2.7 convolution_convert_fusion.3
  316.4 7.5 %fusion.8 = bf16[8,64,4096]{2,1,0:T(8,128)(2,1)} fusion(bf16[8,64,4096]{2,1,0:T(8,128)(2,1)} %collective-permute-done.3, bf16[8,2,64,4096]{3,2,1,0:T(8,128)(2,1)} %bitcast.17, s32[]{:T(128)S(6)} %select_n.47), kind=kLoop, calls=%fused_computation.13 | loop fusion | flops 8388608 | bytes 12582916 | tf_op jit(solution)/shard_map/convert_element_type | solution.py:259
  324.0 18.3 %attend_back_own.1 = (bf16[512,1024]{1,0:T(8,128)(2,1)S(1)}, f32[512,1024]{1,0:T(8,128)S(1)}, f32[512,1024]{1,0:T(8,128)S(1)}) custom-call(bf16[512,1024]{1,0:T(8,128)(2,1)S(1)} %copy-done.9, bf16[512,1024]{1,0:T(8,128)(2,1)S(1)} %copy-done.6, bf16[512,1024]{1,0:T(8,128)(2,1)S(1)} %copy-done.4, f32[512,1024]{1,0:T(8,128)S(1)} %copy-done.12, ...), custom_call_target="tpu_custom_call" | custom-call | flops 10737418240 | bytes 8388608 | tf_op jit(solution)/shard_map/attend_back_own/pallas_call | solution.py:219
  342.3 1.3 copy-done
  343.6 2.3 add_convert_fusion.2
  345.9 14.9 %collective-permute-done.5 = bf16[512,1024]{1,0:T(8,128)(2,1)} collective-permute-done((bf16[512,1024]{1,0:T(8,128)(2,1)}, bf16[512,1024]{1,0:T(8,128)(2,1)}, u32[]{:S(2)}, u32[]{:S(2)}) %collective-permute-start.5) | collective-permute-done | bytes 1048608 | tf_op jit(solution)/shard_map/ppermute | solution.py:389
  360.8 1.6 add_convert_fusion.1
  362.4 6.3 %convolution_convert_fusion.2 = bf16[1024,3072]{1,0:T(8,128)(2,1)} fusion(bf16[512,1024]{1,0:T(8,128)(2,1)S(1)} %add_convert_fusion.1, bf16[512,1024]{1,0:T(8,128)(2,1)S(1)} %add_convert_fusion.2, bf16[512,1024]{1,0:T(8,128)(2,1)S(1)} %get-tuple-element.49, bf16[1,512,1024]{2,1,0:T(8,128)(2,1)S(1)} %copy-done.21, f32[1024]{0:T(1024)S(1)} %reshape.284, ...), kind=kOutput, calls=%fused_computation.21 | convolution fusion | flops 3236954112 | bytes 10498048 | tf_op jit(solution)/shard_map/dot_general | solution.py:35
  369.9 7.1 %fusion.55 = (bf16[1024]{0:T(1024)(128)(2,1)S(1)}, f32[512]{0:T(512)S(1)}, f32[512,1024]{1,0:T(8,128)S(1)}) fusion(f32[1024]{0:T(1024)S(1)} %reshape.283, f32[512]{0:T(512)S(1)} %broadcast_multiply_fusion.1, bf16[1,512,1024]{2,1,0:T(8,128)(2,1)S(1)} %copy-done.22, bf16[1024,4224]{1,0:T(8,128)(2,1)} %all-gather.4.cloned.1.call-done, ...), kind=kOutput, calls=%fused_computation.112 | convolution fusion | flops 3233806848 | bytes 12593152 | tf_op jit(solution)/shard_map/dot_general | solution.py:29
  377.0 1.3 copy-done.23
  378.3 1.0 fusion.28
  379.7 4.4 pad_maximum_fusion
  384.1 2.7 dynamic-slice_bitcast_fusion
  386.8 2.0 copy-done.14
  389.1 7.4 %collective-permute-done.6 = bf16[8,64,4224]{2,1,0:T(8,128)(2,1)} collective-permute-done((bf16[8,64,4224]{2,1,0:T(8,128)(2,1)}, bf16[8,64,4224]{2,1,0:T(8,128)(2,1)}, u32[]{:S(2)}, u32[]{:S(2)}) %collective-permute-start.6) | collective-permute-done | bytes 4325408 | tf_op jit(solution)/shard_map/ppermute | solution.py:257
  396.5 4.6 fusion
  401.4 49.1 %collective-permute-done.7 = bf16[8,32,4224]{2,1,0:T(8,128)(2,1)S(1)} collective-permute-done((bf16[8,32,4224]{2,1,0:T(8,128)(2,1)S(1)}, bf16[8,32,4224]{2,1,0:T(8,128)(2,1)S(1)}, u32[]{:S(2)}, u32[]{:S(2)}) %collective-permute-start.7) | collective-permute-done | bytes 2162720 | tf_op jit(solution)/shard_map/ppermute | solution.py:257
  450.5 1.9 fusion.12
  452.4 22.3 %reduce-scatter.6.cloned.1.call-done = bf16[64,4096]{1,0:T(8,128)(2,1)} async-done(((bf16[512,4096]{1,0:T(8,128)(2,1)}), bf16[64,4096]{1,0:T(8,128)(2,1)}) %reduce-scatter.6.cloned.1.call-update) | async-done | bytes 524304 | tf_op jit(solution)/shard_map/reduce_scatter | solution.py:277
  474.7 11.1 %add_bitcast_fusion.1 = f32[1,512,1024]{2,1,0:T(8,128)} fusion(f32[512,1024]{1,0:T(8,128)} %copy-done.26, bf16[512,4096]{1,0:T(8,128)(2,1)} %copy-done.35, bf16[4096,1024]{1,0:T(8,128)(2,1)} %all-gather.8.cloned.1.call-done, f32[1024]{0:T(1024)S(1)} %reshape.291), kind=kOutput, calls=%fused_computation.61 | convolution fusion | flops 4296015872 | bytes 16781312 | tf_op jit(solution)/shard_map/dot_general | solution.py:41
  485.9 1.5 collective-permute-start.10
  487.9 2.2 add_bitcast_fusion
  490.1 4.9 collective-permute-done.10
  495.1 1.1 maximum_convert_fusion.1
  496.2 50.2 %reduce-scatter.8.cloned.1.call-done = bf16[32,4224]{1,0:T(8,128)(2,1)} async-done(((bf16[256,4224]{1,0:T(8,128)(2,1)}), bf16[32,4224]{1,0:T(8,128)(2,1)}) %reduce-scatter.8.cloned.1.call-update) | async-done | bytes 270352 | tf_op jit(solution)/shard_map/reduce_scatter | solution.py:277
  546.4 1.5 collective-permute-start.8
  547.9 1.1 convert_add_fusion.5
  549.0 4.8 collective-permute-done.8
  553.8 1.0 broadcast_select_fusion.1
  554.8 0.7 maximum_convert_fusion.2
  557.3 0.9 slice.121
  (135 shorter events, 10.2 us)
Async XLA Ops:
  7.2 5.8 %copy-start.19 = (bf16[1,512,1024]{2,1,0:T(8,128)(2,1)S(1)}, bf16[1,512,1024]{2,1,0:T(8,128)(2,1)}, u32[]{:S(2)}) copy-start(bf16[1,512,1024]{2,1,0:T(8,128)(2,1)} %param.14) | copy-start | bytes 3145732
  7.2 83.6 %all-gather.4.cloned.1.call-start = ((), (), s32[]{:S(2)}) async-start(), calls=%async_computation.3 | async-start | bytes 9191424 | tf_op jit(solution)/shard_map/all_gather | solution.py:334
  11.4 161.2 %all-gather.6.cloned.1.call-start = ((), (), s32[]{:S(2)}) async-start(), calls=%async_computation.4 | async-start | bytes 8912896 | tf_op jit(solution)/shard_map/all_gather | solution.py:340
  12.2 229.3 %all-gather.8.cloned.1.call-start = ((), (), s32[]{:S(2)}) async-start(), calls=%async_computation.5 | async-start | bytes 8912896 | tf_op jit(solution)/shard_map/all_gather | solution.py:341
  12.9 330.7 %reduce-scatter.4.cloned.1.call-start = ((), (), s32[]{:S(2)}) async-start(), calls=%async_computation.6 | async-start | bytes 2359296 | tf_op jit(solution)/shard_map/reduce_scatter | solution.py:277
  97.4 48.7 %copy-start.1 = (bf16[512,2048]{1,0:T(8,128)(2,1)}, bf16[512,2048]{1,0:T(8,128)(2,1)S(1)}, u32[]{:S(2)}) copy-start(bf16[512,2048]{1,0:T(8,128)(2,1)S(1)} %add_convert_fusion.k_ref.v_ref) | copy-start | bytes 6291460
  97.4 48.7 %collective-permute-start = (bf16[512,2048]{1,0:T(8,128)(2,1)S(1)}, bf16[512,2048]{1,0:T(8,128)(2,1)}, u32[]{:S(2)}, u32[]{:S(2)}) collective-permute-start(bf16[512,2048]{1,0:T(8,128)(2,1)S(1)} %add_convert_fusion.k_ref.v_ref), channel_id=1, source_target_pairs={{0,1},{2,3},{4,5},{6,7},{8,9},{10,11},{12,13},{14,15},{16,17},{18,... | collective-permute-start | bytes 6291464 | tf_op jit(solution)/shard_map/ppermute | solution.py:354
  105.3 62.8 %copy-start.7 = (bf16[512,1024]{1,0:T(8,128)(2,1)}, bf16[512,1024]{1,0:T(8,128)(2,1)S(1)}, u32[]{:S(2)}) copy-start(bf16[512,1024]{1,0:T(8,128)(2,1)S(1)} %add_convert_fusion.4.q_ref) | copy-start | bytes 3145732
  146.1 22.1 %copy-start.20 = (bf16[1,512,1024]{2,1,0:T(8,128)(2,1)S(1)}, bf16[1,512,1024]{2,1,0:T(8,128)(2,1)}, u32[]{:S(2)}) copy-start(bf16[1,512,1024]{2,1,0:T(8,128)(2,1)} %param.14) | copy-start | bytes 3145732
  168.1 4.1 copy-start.10
  168.1 145.6 %copy-start.3 = (bf16[512,1024]{1,0:T(8,128)(2,1)}, bf16[512,1024]{1,0:T(8,128)(2,1)S(1)}, u32[]{:S(2)}) copy-start(bf16[512,1024]{1,0:T(8,128)(2,1)S(1)} %get-tuple-element.36.ctx_ref) | copy-start | bytes 3145732
  172.2 111.7 %copy-start.26 = (f32[512,1024]{1,0:T(8,128)}, f32[512,1024]{1,0:T(8,128)S(1)}, u32[]{:S(2)}) copy-start(f32[512,1024]{1,0:T(8,128)S(1)} %get-tuple-element.89) | copy-start | bytes 6291460
  172.6 13.0 %copy-start.27 = (bf16[1,512,1024]{2,1,0:T(8,128)(2,1)S(1)}, bf16[1,512,1024]{2,1,0:T(8,128)(2,1)}, u32[]{:S(2)}) copy-start(bf16[1,512,1024]{2,1,0:T(8,128)(2,1)} %param.15) | copy-start | bytes 3145732
  185.7 4.8 copy-start.35
  190.5 3.3 copy-start.25
  196.6 7.5 %collective-permute-start.1 = (bf16[8,256,1024]{2,1,0:T(8,128)(2,1)}, bf16[8,256,1024]{2,1,0:T(8,128)(2,1)}, u32[]{:S(2)}, u32[]{:S(2)}) collective-permute-start(bf16[8,256,1024]{2,1,0:T(8,128)(2,1)} %dynamic-slice_bitcast_fusion.2), channel_id=1, source_target_pairs={{0,2},{2,0},{4,6},{6,4},{8,10},{10,8},{12,14},{14,12},{16,18},{18,... | collective-permute-start | bytes 12582920 | tf_op jit(solution)/shard_map/ppermute | solution.py:257
  209.7 2.0 copy-start.17
  213.3 52.5 %collective-permute-start.2 = (bf16[8,128,1024]{2,1,0:T(8,128)(2,1)}, bf16[8,128,1024]{2,1,0:T(8,128)(2,1)}, u32[]{:S(2)}, u32[]{:S(2)}) collective-permute-start(bf16[8,128,1024]{2,1,0:T(8,128)(2,1)} %dynamic-slice_bitcast_fusion.4), channel_id=1, source_target_pairs={{0,1},{1,0},{2,3},{3,2},{4,5},{5,4},{6,7},{7,6},{8,9},{9,8},{10,11... | collective-permute-start | bytes 6291464 | tf_op jit(solution)/shard_map/ppermute | solution.py:257
  256.4 9.4 %copy-start.18 = (bf16[8,256,1024]{2,1,0:T(8,128)(2,1)S(1)}, bf16[8,256,1024]{2,1,0:T(8,128)(2,1)}, u32[]{:S(2)}) copy-start(bf16[8,256,1024]{2,1,0:T(8,128)(2,1)} %copy-done.17) | copy-start | bytes 12582916
  274.4 42.0 %collective-permute-start.3 = (bf16[8,64,4096]{2,1,0:T(8,128)(2,1)}, bf16[8,64,4096]{2,1,0:T(8,128)(2,1)}, u32[]{:S(2)}, u32[]{:S(2)}) collective-permute-start(bf16[8,64,4096]{2,1,0:T(8,128)(2,1)} %dynamic-slice_bitcast_fusion.1), channel_id=1, source_target_pairs={{0,2},{2,0},{4,6},{6,4},{8,10},{10,8},{12,14},{14,12},{16,18},{18,... | collective-permute-start | bytes 12582920 | tf_op jit(solution)/shard_map/ppermute | solution.py:257
  274.7 199.9 %reduce-scatter.6.cloned.1.call-start = ((), (), s32[]{:S(2)}) async-start(), calls=%async_computation.7 | async-start | bytes 4718592 | tf_op jit(solution)/shard_map/reduce_scatter | solution.py:277
  284.0 1.2 copy-start.28
  284.7 4.2 copy-start.15
  285.8 3.1 copy-start.8
  285.8 3.1 copy-start.11
  288.9 20.6 %copy-start.5 = (bf16[512,1024]{1,0:T(8,128)(2,1)}, bf16[512,1024]{1,0:T(8,128)(2,1)S(1)}, u32[]{:S(2)}) copy-start(bf16[512,1024]{1,0:T(8,128)(2,1)S(1)} %fusion.40.g_ref) | copy-start | bytes 3145732
  309.4 1.4 copy-start.13
  310.8 32.8 %collective-permute-start.4 = (bf16[512,1024]{1,0:T(8,128)(2,1)}, bf16[512,1024]{1,0:T(8,128)(2,1)}, u32[]{:S(2)}, u32[]{:S(2)}) collective-permute-start(bf16[512,1024]{1,0:T(8,128)(2,1)} %get-tuple-element.51), channel_id=1, source_target_pairs={{1,0},{3,2},{5,4},{7,6},{9,8},{11,10},{13,12},{15,14},{17,16},{19,... | collective-permute-start | bytes 3145736 | tf_op jit(solution)/shard_map/ppermute | solution.py:388
  312.1 48.7 %collective-permute-start.5 = (bf16[512,1024]{1,0:T(8,128)(2,1)}, bf16[512,1024]{1,0:T(8,128)(2,1)}, u32[]{:S(2)}, u32[]{:S(2)}) collective-permute-start(bf16[512,1024]{1,0:T(8,128)(2,1)} %get-tuple-element.53), channel_id=1, source_target_pairs={{1,0},{3,2},{5,4},{7,6},{9,8},{11,10},{13,12},{15,14},{17,16},{19,... | collective-permute-start | bytes 3145736 | tf_op jit(solution)/shard_map/ppermute | solution.py:389
  316.4 7.5 %copy-start.2 = (bf16[512,2048]{1,0:T(8,128)(2,1)S(1)}, bf16[512,2048]{1,0:T(8,128)(2,1)}, u32[]{:S(2)}) copy-start(bf16[512,2048]{1,0:T(8,128)(2,1)} %copy-done.1) | copy-start | bytes 6291460
  316.4 7.5 %copy-start.4 = (bf16[512,1024]{1,0:T(8,128)(2,1)S(1)}, bf16[512,1024]{1,0:T(8,128)(2,1)}, u32[]{:S(2)}) copy-start(bf16[512,1024]{1,0:T(8,128)(2,1)} %copy-done.3) | copy-start | bytes 3145732
  316.4 7.5 %copy-start.6 = (bf16[512,1024]{1,0:T(8,128)(2,1)S(1)}, bf16[512,1024]{1,0:T(8,128)(2,1)}, u32[]{:S(2)}) copy-start(bf16[512,1024]{1,0:T(8,128)(2,1)} %copy-done.5) | copy-start | bytes 3145732
  316.4 7.5 %copy-start.9 = (bf16[512,1024]{1,0:T(8,128)(2,1)S(1)}, bf16[512,1024]{1,0:T(8,128)(2,1)}, u32[]{:S(2)}) copy-start(bf16[512,1024]{1,0:T(8,128)(2,1)} %copy-done.7) | copy-start | bytes 3145732
  316.4 7.5 %copy-start.12 = (f32[512,1024]{1,0:T(8,128)S(1)}, f32[512,1024]{1,0:T(8,128)}, u32[]{:S(2)}) copy-start(f32[512,1024]{1,0:T(8,128)} %copy-done.10) | copy-start | bytes 6291460
  342.3 1.3 copy-start
  343.6 18.8 %copy-start.21 = (bf16[1,512,1024]{2,1,0:T(8,128)(2,1)S(1)}, bf16[1,512,1024]{2,1,0:T(8,128)(2,1)}, u32[]{:S(2)}) copy-start(bf16[1,512,1024]{2,1,0:T(8,128)(2,1)} %param.14) | copy-start | bytes 3145732
  345.9 22.8 %copy-start.30 = (bf16[512,1024]{1,0:T(8,128)(2,1)}, bf16[512,1024]{1,0:T(8,128)(2,1)S(1)}, u32[]{:S(2)}) copy-start(bf16[512,1024]{1,0:T(8,128)(2,1)S(1)} %add_convert_fusion.2) | copy-start | bytes 3145732
  362.4 6.3 %copy-start.31 = (bf16[512,1024]{1,0:T(8,128)(2,1)}, bf16[512,1024]{1,0:T(8,128)(2,1)S(1)}, u32[]{:S(2)}) copy-start(bf16[512,1024]{1,0:T(8,128)(2,1)S(1)} %add_convert_fusion.1) | copy-start | bytes 3145732
  368.7 1.2 copy-start.22
  377.0 1.3 copy-start.23
  384.1 4.7 copy-start.14
  388.8 7.7 %collective-permute-start.6 = (bf16[8,64,4224]{2,1,0:T(8,128)(2,1)}, bf16[8,64,4224]{2,1,0:T(8,128)(2,1)}, u32[]{:S(2)}, u32[]{:S(2)}) collective-permute-start(bf16[8,64,4224]{2,1,0:T(8,128)(2,1)} %dynamic-slice_bitcast_fusion), channel_id=1, source_target_pairs={{0,2},{2,0},{4,6},{6,4},{8,10},{10,8},{12,14},{14,12},{16,18},{18,... | collective-permute-start | bytes 12976136 | tf_op jit(solution)/shard_map/ppermute | solution.py:257
  388.9 157.5 %reduce-scatter.8.cloned.1.call-start = ((), (), s32[]{:S(2)}) async-start(), calls=%async_computation.8 | async-start | bytes 2433024 | tf_op jit(solution)/shard_map/reduce_scatter | solution.py:277
  401.3 73.3 %copy-start.34 = (f32[16,64]{1,0:T(8,128)S(1)}, f32[16,64]{1,0:T(8,128)}, u32[]{:S(2)}) copy-start(f32[16,64]{1,0:T(8,128)} %get-tuple-element.76) | copy-start | bytes 12292
  401.3 49.1 %collective-permute-start.7 = (bf16[8,32,4224]{2,1,0:T(8,128)(2,1)S(1)}, bf16[8,32,4224]{2,1,0:T(8,128)(2,1)S(1)}, u32[]{:S(2)}, u32[]{:S(2)}) collective-permute-start(bf16[8,32,4224]{2,1,0:T(8,128)(2,1)S(1)} %dynamic-slice_bitcast_fusion.3), channel_id=1, source_target_pairs={{0,1},{1,0},{2,3},{3,2},{4,5},{5,4},{6,7},{7,6},{8,9},{9,8},{10,11... | collective-permute-start | bytes 6488072 | tf_op jit(solution)/shard_map/ppermute | solution.py:257
  474.7 11.2 %copy-start.33 = (bf16[128,1024]{1,0:T(8,128)(2,1)S(1)}, bf16[128,1024]{1,0:T(8,128)(2,1)}, u32[]{:S(2)}) copy-start(bf16[128,1024]{1,0:T(8,128)(2,1)} %reduce-scatter.4.cloned.1.call-done) | copy-start | bytes 786436
  474.7 12.6 %copy-start.32 = (bf16[64,4096]{1,0:T(8,128)(2,1)S(1)}, bf16[64,4096]{1,0:T(8,128)(2,1)}, u32[]{:S(2)}) copy-start(bf16[64,4096]{1,0:T(8,128)(2,1)} %reduce-scatter.6.cloned.1.call-done) | copy-start | bytes 1572868
  474.7 13.2 %copy-start.16 = (f32[512,1024]{1,0:T(8,128)S(1)}, f32[512,1024]{1,0:T(8,128)}, u32[]{:S(2)}) copy-start(f32[512,1024]{1,0:T(8,128)} %copy-done.15) | copy-start | bytes 6291460
  474.7 13.2 %copy-start.24 = (f32[512,1024]{1,0:T(8,128)S(1)}, f32[512,1024]{1,0:T(8,128)}, u32[]{:S(2)}) copy-start(f32[512,1024]{1,0:T(8,128)} %copy-done.23) | copy-start | bytes 6291460
  474.7 13.2 %copy-start.29 = (bf16[1,512,1024]{2,1,0:T(8,128)(2,1)S(1)}, bf16[1,512,1024]{2,1,0:T(8,128)(2,1)}, u32[]{:S(2)}) copy-start(bf16[1,512,1024]{2,1,0:T(8,128)(2,1)} %param.15) | copy-start | bytes 3145732
  485.9 9.2 %collective-permute-start.10 = (bf16[128,1024]{1,0:T(8,128)(2,1)S(1)}, bf16[128,1024]{1,0:T(8,128)(2,1)S(1)}, u32[]{:S(2)}, u32[]{:S(2)}) collective-permute-start(bf16[128,1024]{1,0:T(8,128)(2,1)S(1)} %copy-done.33), channel_id=1, source_target_pairs={{0,1},{1,0},{2,3},{3,2},{4,5},{5,4},{6,7},{7,6},{8,9},{9,8},{10,11... | collective-permute-start | bytes 786440 | tf_op jit(solution)/shard_map/ppermute | solution.py:289
  487.4 60.5 %collective-permute-start.9 = (bf16[64,4096]{1,0:T(8,128)(2,1)S(1)}, bf16[64,4096]{1,0:T(8,128)(2,1)S(1)}, u32[]{:S(2)}, u32[]{:S(2)}) collective-permute-start(bf16[64,4096]{1,0:T(8,128)(2,1)S(1)} %copy-done.32), channel_id=1, source_target_pairs={{0,1},{1,0},{2,3},{3,2},{4,5},{5,4},{6,7},{7,6},{8,9},{9,8},{10,11... | collective-permute-start | bytes 1572872 | tf_op jit(solution)/shard_map/ppermute | solution.py:289
  546.4 7.4 %collective-permute-start.8 = (bf16[32,4224]{1,0:T(8,128)(2,1)}, bf16[32,4224]{1,0:T(8,128)(2,1)S(1)}, u32[]{:S(2)}, u32[]{:S(2)}) collective-permute-start(bf16[32,4224]{1,0:T(8,128)(2,1)} %reduce-scatter.8.cloned.1.call-done), channel_id=1, source_target_pairs={{0,1},{1,0},{2,3},{3,2},{4,5},{5,4},{6,7},{7,6},{8,9},{9,8},{10,11... | collective-permute-start | bytes 811016 | tf_op jit(solution)/shard_map/ppermute | solution.py:289
Sparse Core Ops, SparseCore 0:
  11.6 79.2 all-gather.3
  93.0 73.0 all-gather.5
  168.3 73.1 all-gather.7
  274.8 65.9 reduce-scatter.3
  389.0 85.5 reduce-scatter.5
  478.3 67.9 reduce-scatter.7

commit v3 on v2

--- a/solution.py
+++ b/solution.py
@@ -422,10 +422,9 @@
     small_part = pack_rows(
         [part.astype(bf16).reshape(shards, -1) for part in small_parts], rows
     )
-    attn_held = sum_ranks(
-        sum_cores(jnp.concatenate([qkv_part, out_part, small_part], 1), shards), ranks
-    )
+    attn_held = sum_cores(jnp.concatenate([qkv_part, out_part, small_part], 1), shards)
     up_owned, attn_held = lax.optimization_barrier((up_owned, attn_held))
+    attn_held = sum_ranks(attn_held, ranks)
     attn_owned = sum_chips(attn_held, shards)
     upmatrix_grad = finish_sum(up_owned, ranks, False)
     downmatrix_grad = finish_sum(down_owned, ranks, True)

time: 570 us -> 600 us (1.053)
  waiting for transfers between devices: 306 us -> 344 us
    reduce_scatter x3, waiting for transfers between devices: 72.4 us -> 111 us  [sum_chips(): lax.psum_scatter(held.reshape(-1, held.shape[-1]), 'dp', scatter_dimensio...]
    unnamed x75 -> x79, local copies, waits for them, and re-layouts: 12.6 us -> 7.66 us
  transfers between devices with their start and end apart: 17 -> 17, of which waited for: 11 -> 11; matrix products, arithmetic and copies ran while one was open for 20% -> 20% of each run, Pallas kernels for 11% -> 10%
where the time goes in v3:
time: 600 us; the launch traced here: 596 us
  waiting for transfers between devices  344 us (57%)
  matrix products  92.7 us (15%)
  Pallas kernels  61.4 us (10%)
  other arithmetic  40.9 us (7%)
  local copies, waits for them, and re-layouts  26.7 us (4%)
  starting transfers between devices  15.6 us (3%)
  between operations  14.9 us (2%)
    reduce_scatter x3, waiting for transfers between devices, sum_chips(): lax.psum_scatter(held.reshape(-1, held.shape[-1]), 'dp', scatter_dimensio...  111 us
    all_gather x1, waiting for transfers between devices, local(): lax.all_gather(jnp.concatenate([query_key_value_matrix, attention_exit_ma...  77.2 us
    ppermute x5, waiting for transfers between devices, swap_half(): other = lax.ppermute(pick(blocks, 1 - mine), axis, pairs)  62.2 us
    ppermute x1, waiting for transfers between devices, local(): far = lax.ppermute(keyvals, 'seq', [(0, 1)])  40.8 us
    dot_general x5, matrix products, dot_nn(): return jnp.dot(left, right, preferred_element_type=jnp.float32)  35.8 us
    dot_general x4, matrix products, dot_nt(): lax.dot_general(left, right, (((1,), (1,)), ((), ())), preferred_element_...  35 us
    all_gather x1, waiting for transfers between devices, local(): lax.all_gather(contract_projection_matrix, 'dp', axis=0, tiled=True)  27 us
    pallas_call x1, Pallas kernels, attend(): pl.pallas_call(forward_kernel, grid=(pairs,), in_specs=[LIMIT_SPEC, pair_...  22.3 us
  transfers between devices with their start and end apart: 17, of which 11 were waited for; matrix products, arithmetic and copies ran while one was open for 20% of the time, Pallas kernels for 10%

profile of v3, /device:TPU:0, one launch (start us, length us, event | category | flops | bytes accessed | tf_op | source)
XLA Modules:
  0.0 596.0 jit_solution(8757749337684257806)
XLA Ops:
  7.2 0.7 broadcast_in_dim.51
  8.6 0.8 concatenate.28
  9.5 1.9 pad_maximum_fusion.2
  13.6 77.2 %all-gather.4.cloned.1.call-done = bf16[1024,4224]{1,0:T(8,128)(2,1)} async-done(((bf16[64,4224]{1,0:T(8,128)(2,1)}), bf16[1024,4224]{1,0:T(8,128)(2,1)}) %all-gather.4.cloned.1.call-update) | async-done | bytes 8650768 | tf_op jit(solution)/shard_map/all_gather | solution.py:334
  90.8 1.0 slice.104
  92.7 4.6 add_convert_fusion.k_ref.v_ref
  97.4 4.8 collective-permute-start
  102.4 2.9 add_convert_fusion.4.q_ref
  105.3 40.8 %collective-permute-done.kr_ref.vr_ref = bf16[512,2048]{1,0:T(8,128)(2,1)} collective-permute-done((bf16[512,2048]{1,0:T(8,128)(2,1)S(1)}, bf16[512,2048]{1,0:T(8,128)(2,1)}, u32[]{:S(2)}, u32[]{:S(2)}) %collective-permute-start) | collective-permute-done | bytes 2097184 | tf_op jit(solution)/shard_map/ppermute | solution.py:354
  146.1 22.3 %attend.1 = (bf16[512,1024]{1,0:T(8,128)(2,1)S(1)}, f32[512,1024]{1,0:T(8,128)S(1)}) custom-call(s32[1]{0:T(128)} %bitcast.1.limit_ref, bf16[512,1024]{1,0:T(8,128)(2,1)S(1)} %add_convert_fusion.4.q_ref, bf16[512,2048]{1,0:T(8,128)(2,1)S(1)} %add_convert_fusion.k_ref.v_ref, bf16[512,2048]{1,0:T(8,128)(2,1)S(1)} %add_convert_fusion.k_ref.v_ref, ...), custom_call_target="tpu_custom_call" | custom-call | flops 8589934592 | bytes 12582912 | tf_op jit(solution)/shard_map/attend/pallas_call | solution.py:172
  168.4 4.1 fusion.61
  172.9 13.0 %multiply_convert_fusion = (bf16[512,4096]{1,0:T(8,128)(2,1)S(1)}, f32[512,4096]{1,0:T(8,128)}) fusion(f32[4096]{0:T(1024)S(1)} %bitcast.146, bf16[1024,4096]{1,0:T(8,128)(2,1)} %all-gather.6.cloned.1.call-done, f32[512,1024]{1,0:T(8,128)S(1)} %get-tuple-element.89, f32[1024]{0:T(1024)S(1)} %reshape.288, f32[1024]{0:T(1024)S(1)} %reshape.287, ...), kind=kOutput, calls=%fused_computation.16 | convolution fusion | flops 4318560256 | bytes 23097344 | tf_op jit(solution)/shard_map/dot_general | solution.py:41
  185.9 4.8 convolution_convert_fusion.1
  190.8 3.4 dynamic-slice_bitcast_fusion.2
  194.1 1.1 copy-done.24
  195.3 7.5 %collective-permute-done.1 = bf16[8,256,1024]{2,1,0:T(8,128)(2,1)} collective-permute-done((bf16[8,256,1024]{2,1,0:T(8,128)(2,1)}, bf16[8,256,1024]{2,1,0:T(8,128)(2,1)}, u32[]{:S(2)}, u32[]{:S(2)}) %collective-permute-start.1) | collective-permute-done | bytes 4194336 | tf_op jit(solution)/shard_map/ppermute | solution.py:257
  202.8 5.6 fusion.9
  208.4 2.0 copy-done.17
  210.4 1.5 dynamic-slice_bitcast_fusion.4
  212.0 2.5 collective-permute-start.2
  214.5 27.0 %all-gather.8.cloned.1.call-done = bf16[4096,1024]{1,0:T(8,128)(2,1)} async-done(((bf16[256,1024]{1,0:T(8,128)(2,1)}), bf16[4096,1024]{1,0:T(8,128)(2,1)}) %all-gather.8.cloned.1.call-update) | async-done | bytes 8388624 | tf_op jit(solution)/shard_map/all_gather | solution.py:341
  241.5 14.8 %fusion.56 = (bf16[4096]{0:T(1024)(128)(2,1)S(1)}, bf16[512,4096]{1,0:T(8,128)(2,1)}) fusion(f32[512,4096]{1,0:T(8,128)} %get-tuple-element.91, f32[4096]{0:T(1024)S(1)} %bitcast.147, bf16[512,1024]{1,0:T(8,128)(2,1)} %bitcast.137, bf16[4096,1024]{1,0:T(8,128)(2,1)} %all-gather.8.cloned.1.call-done), kind=kOutput, calls=%fused_computation.113 | convolution fusion | flops 4341100544 | bytes 22044672 | tf_op jit(solution)/shard_map/dot_general | solution.py:29
  256.3 9.3 %convolution_convert_fusion = bf16[1024,4096]{1,0:T(8,128)(2,1)} fusion(bf16[512,4096]{1,0:T(8,128)(2,1)} %get-tuple-element.40, f32[512,1024]{1,0:T(8,128)S(1)} %get-tuple-element.89, f32[1024]{0:T(1024)S(1)} %reshape.288, f32[1024]{0:T(1024)S(1)} %reshape.287, f32[512]{0:T(512)S(1)} %fusion.47, f32[512]{0:T(512)S(1)} %broadcast_multiply_fusion), kind=kOutput, calls=%fused_computation.17 | convolution fusion | flops 4301783040 | bytes 14692352 | tf_op jit(solution)/shard_map/dot_general | solution.py:35
  265.7 3.9 fusion.15
  269.5 4.7 dynamic-slice_bitcast_fusion.1
  274.5 8.9 %multiply_reduce_fusion = (bf16[1024]{0:T(1024)(128)(2,1)S(1)}, f32[512]{0:T(512)S(1)}, bf16[1024]{0:T(1024)(128)(2,1)S(1)}, f32[512,1024]{1,0:T(8,128)S(1)}) fusion(f32[512,1024]{1,0:T(8,128)S(1)} %get-tuple-element.89, f32[512]{0:T(512)S(1)} %fusion.47, f32[512]{0:T(512)S(1)} %broadcast_multiply_fusion, f32[1024]{0:T(1024)S(1)} %reshape.287, ...), kind=kOutput, calls=%fused_computation.54 | convolution fusion | flops 4299159040 | bytes 16791552 | tf_op jit(solution)/shard_map/dot_general | solution.py:29
  283.5 0.7 fusion.60
  285.3 3.0 fusion.40.g_ref
  288.4 20.6 %attend_back_far.1 = (f32[512,1024]{1,0:T(8,128)S(1)}, bf16[512,1024]{1,0:T(8,128)(2,1)}, bf16[512,1024]{1,0:T(8,128)(2,1)}) custom-call(s32[1]{0:T(128)} %bitcast.1.limit_ref, bf16[512,1024]{1,0:T(8,128)(2,1)S(1)} %copy-done.8, bf16[512,1024]{1,0:T(8,128)(2,1)S(1)} %fusion.40.g_ref, bf16[512,1024]{1,0:T(8,128)(2,1)S(1)} %get-tuple-element.36.ctx_ref, ...), custom_call_target="tpu_custom_call" | custom-call | flops 10737418240 | bytes 8388608 | tf_op jit(solution)/shard_map/attend_back_far/pallas_call | solution.py:198
  309.0 1.3 copy-done.13
  310.4 1.3 collective-permute-start.4
  311.7 1.3 collective-permute-start.5
  313.3 2.7 convolution_convert_fusion.3
  316.0 7.4 %fusion.8 = bf16[8,64,4096]{2,1,0:T(8,128)(2,1)} fusion(bf16[8,64,4096]{2,1,0:T(8,128)(2,1)} %collective-permute-done.3, bf16[8,2,64,4096]{3,2,1,0:T(8,128)(2,1)} %bitcast.17, s32[]{:T(128)S(6)} %select_n.47), kind=kLoop, calls=%fused_computation.13 | loop fusion | flops 8388608 | bytes 12582916 | tf_op jit(solution)/shard_map/convert_element_type | solution.py:259
  323.4 18.5 %attend_back_own.1 = (bf16[512,1024]{1,0:T(8,128)(2,1)S(1)}, f32[512,1024]{1,0:T(8,128)S(1)}, f32[512,1024]{1,0:T(8,128)S(1)}) custom-call(bf16[512,1024]{1,0:T(8,128)(2,1)S(1)} %copy-done.9, bf16[512,1024]{1,0:T(8,128)(2,1)S(1)} %copy-done.6, bf16[512,1024]{1,0:T(8,128)(2,1)S(1)} %copy-done.4, f32[512,1024]{1,0:T(8,128)S(1)} %copy-done.12, ...), custom_call_target="tpu_custom_call" | custom-call | flops 10737418240 | bytes 8388608 | tf_op jit(solution)/shard_map/attend_back_own/pallas_call | solution.py:219
  342.0 1.3 copy-done
  343.3 2.3 add_convert_fusion.2
  345.6 14.7 %collective-permute-done.5 = bf16[512,1024]{1,0:T(8,128)(2,1)} collective-permute-done((bf16[512,1024]{1,0:T(8,128)(2,1)}, bf16[512,1024]{1,0:T(8,128)(2,1)}, u32[]{:S(2)}, u32[]{:S(2)}) %collective-permute-start.5) | collective-permute-done | bytes 1048608 | tf_op jit(solution)/shard_map/ppermute | solution.py:389
  360.4 1.6 add_convert_fusion.1
  362.0 8.2 %fusion.55 = (bf16[1024]{0:T(1024)(128)(2,1)S(1)}, f32[512]{0:T(512)S(1)}, f32[512,1024]{1,0:T(8,128)}) fusion(f32[1024]{0:T(1024)S(1)} %reshape.283, f32[512]{0:T(512)S(1)} %broadcast_multiply_fusion.1, bf16[1,512,1024]{2,1,0:T(8,128)(2,1)S(1)} %copy-done.21, bf16[1024,4224]{1,0:T(8,128)(2,1)} %all-gather.4.cloned.1.call-done, ...), kind=kOutput, calls=%fused_computation.112 | convolution fusion | flops 3233806848 | bytes 12593152 | tf_op jit(solution)/shard_map/dot_general | solution.py:29
  370.3 1.1 copy-done.22
  371.4 2.6 fusion.28
  374.0 0.7 fusion.49
  375.2 5.1 convolution_convert_fusion.2
  380.2 0.8 pad_maximum_fusion
  381.6 7.3 %collective-permute-done.6 = bf16[8,64,4224]{2,1,0:T(8,128)(2,1)S(1)} collective-permute-done((bf16[8,64,4224]{2,1,0:T(8,128)(2,1)S(1)}, bf16[8,64,4224]{2,1,0:T(8,128)(2,1)S(1)}, u32[]{:S(2)}, u32[]{:S(2)}) %collective-permute-start.6) | collective-permute-done | bytes 4325408 | tf_op jit(solution)/shard_map/ppermute | solution.py:257
  388.9 3.1 fusion
  392.0 63.7 %reduce-scatter.6.cloned.1.call-done = bf16[64,4096]{1,0:T(8,128)(2,1)} async-done(((bf16[512,4096]{1,0:T(8,128)(2,1)}), bf16[64,4096]{1,0:T(8,128)(2,1)}) %reduce-scatter.6.cloned.1.call-update) | async-done | bytes 524304 | tf_op jit(solution)/shard_map/reduce_scatter | solution.py:277
  455.7 1.9 dynamic-slice_bitcast_fusion.3
  457.6 1.5 collective-permute-start.7
  459.2 47.3 %collective-permute-done.7 = bf16[8,32,4224]{2,1,0:T(8,128)(2,1)S(1)} collective-permute-done((bf16[8,32,4224]{2,1,0:T(8,128)(2,1)S(1)}, bf16[8,32,4224]{2,1,0:T(8,128)(2,1)S(1)}, u32[]{:S(2)}, u32[]{:S(2)}) %collective-permute-start.7) | collective-permute-done | bytes 2162720 | tf_op jit(solution)/shard_map/ppermute | solution.py:257
  506.5 1.9 fusion.12
  508.5 11.1 %add_bitcast_fusion.1 = f32[1,512,1024]{2,1,0:T(8,128)} fusion(f32[512,1024]{1,0:T(8,128)} %copy-done.25, bf16[512,4096]{1,0:T(8,128)(2,1)} %copy-done.37, bf16[4096,1024]{1,0:T(8,128)(2,1)} %all-gather.8.cloned.1.call-done, f32[1024]{0:T(1024)S(1)} %reshape.291), kind=kOutput, calls=%fused_computation.61 | convolution fusion | flops 4296015872 | bytes 16781312 | tf_op jit(solution)/shard_map/dot_general | solution.py:41
  519.7 1.6 collective-permute-start.10
  521.7 2.2 add_bitcast_fusion
  523.9 5.0 collective-permute-done.10
  529.0 1.1 maximum_convert_fusion.1
  530.1 46.9 %reduce-scatter.8.cloned.1.call-done = bf16[32,4224]{1,0:T(8,128)(2,1)} async-done(((bf16[256,4224]{1,0:T(8,128)(2,1)}), bf16[32,4224]{1,0:T(8,128)(2,1)}) %reduce-scatter.8.cloned.1.call-update) | async-done | bytes 270352 | tf_op jit(solution)/shard_map/reduce_scatter | solution.py:277
  577.0 1.6 collective-permute-start.8
  578.6 1.1 convert_add_fusion.5
  579.7 4.8 collective-permute-done.8
  584.5 1.0 broadcast_select_fusion.1
  585.5 0.7 maximum_convert_fusion.2
  588.0 0.9 slice.121
  (139 shorter events, 9.7 us)
Async XLA Ops:
  7.2 5.8 copy-start.19
  7.2 83.6 %all-gather.4.cloned.1.call-start = ((), (), s32[]{:S(2)}) async-start(), calls=%async_computation.3 | async-start | bytes 9191424 | tf_op jit(solution)/shard_map/all_gather | solution.py:334
  11.4 161.5 %all-gather.6.cloned.1.call-start = ((), (), s32[]{:S(2)}) async-start(), calls=%async_computation.4 | async-start | bytes 8912896 | tf_op jit(solution)/shard_map/all_gather | solution.py:340
  12.2 229.3 %all-gather.8.cloned.1.call-start = ((), (), s32[]{:S(2)}) async-start(), calls=%async_computation.5 | async-start | bytes 8912896 | tf_op jit(solution)/shard_map/all_gather | solution.py:341
  12.9 330.4 %reduce-scatter.4.cloned.1.call-start = ((), (), s32[]{:S(2)}) async-start(), calls=%async_computation.6 | async-start | bytes 2359296 | tf_op jit(solution)/shard_map/reduce_scatter | solution.py:277
  97.4 48.7 %copy-start.1 = (bf16[512,2048]{1,0:T(8,128)(2,1)}, bf16[512,2048]{1,0:T(8,128)(2,1)S(1)}, u32[]{:S(2)}) copy-start(bf16[512,2048]{1,0:T(8,128)(2,1)S(1)} %add_convert_fusion.k_ref.v_ref) | copy-start | bytes 6291460
  97.4 48.7 %collective-permute-start = (bf16[512,2048]{1,0:T(8,128)(2,1)S(1)}, bf16[512,2048]{1,0:T(8,128)(2,1)}, u32[]{:S(2)}, u32[]{:S(2)}) collective-permute-start(bf16[512,2048]{1,0:T(8,128)(2,1)S(1)} %add_convert_fusion.k_ref.v_ref), channel_id=1, source_target_pairs={{0,1},{2,3},{4,5},{6,7},{8,9},{10,11},{12,13},{14,15},{16,17},{18,... | collective-permute-start | bytes 6291464 | tf_op jit(solution)/shard_map/ppermute | solution.py:354
  105.3 63.1 %copy-start.7 = (bf16[512,1024]{1,0:T(8,128)(2,1)}, bf16[512,1024]{1,0:T(8,128)(2,1)S(1)}, u32[]{:S(2)}) copy-start(bf16[512,1024]{1,0:T(8,128)(2,1)S(1)} %add_convert_fusion.4.q_ref) | copy-start | bytes 3145732
  146.1 22.3 %copy-start.20 = (bf16[1,512,1024]{2,1,0:T(8,128)(2,1)S(1)}, bf16[1,512,1024]{2,1,0:T(8,128)(2,1)}, u32[]{:S(2)}) copy-start(bf16[1,512,1024]{2,1,0:T(8,128)(2,1)} %param.14) | copy-start | bytes 3145732
  168.4 4.1 copy-start.10
  168.4 144.9 %copy-start.3 = (bf16[512,1024]{1,0:T(8,128)(2,1)}, bf16[512,1024]{1,0:T(8,128)(2,1)S(1)}, u32[]{:S(2)}) copy-start(bf16[512,1024]{1,0:T(8,128)(2,1)S(1)} %get-tuple-element.36.ctx_ref) | copy-start | bytes 3145732
  172.5 111.0 %copy-start.25 = (f32[512,1024]{1,0:T(8,128)}, f32[512,1024]{1,0:T(8,128)S(1)}, u32[]{:S(2)}) copy-start(f32[512,1024]{1,0:T(8,128)S(1)} %get-tuple-element.89) | copy-start | bytes 6291460
  172.9 13.0 %copy-start.26 = (bf16[1,512,1024]{2,1,0:T(8,128)(2,1)S(1)}, bf16[1,512,1024]{2,1,0:T(8,128)(2,1)}, u32[]{:S(2)}) copy-start(bf16[1,512,1024]{2,1,0:T(8,128)(2,1)} %param.15) | copy-start | bytes 3145732
  185.9 4.8 copy-start.37
  190.7 4.5 copy-start.24
  195.3 7.5 %collective-permute-start.1 = (bf16[8,256,1024]{2,1,0:T(8,128)(2,1)}, bf16[8,256,1024]{2,1,0:T(8,128)(2,1)}, u32[]{:S(2)}, u32[]{:S(2)}) collective-permute-start(bf16[8,256,1024]{2,1,0:T(8,128)(2,1)} %dynamic-slice_bitcast_fusion.2), channel_id=1, source_target_pairs={{0,2},{2,0},{4,6},{6,4},{8,10},{10,8},{12,14},{14,12},{16,18},{18,... | collective-permute-start | bytes 12582920 | tf_op jit(solution)/shard_map/ppermute | solution.py:257
  208.4 2.1 copy-start.17
  212.0 53.7 %collective-permute-start.2 = (bf16[8,128,1024]{2,1,0:T(8,128)(2,1)}, bf16[8,128,1024]{2,1,0:T(8,128)(2,1)}, u32[]{:S(2)}, u32[]{:S(2)}) collective-permute-start(bf16[8,128,1024]{2,1,0:T(8,128)(2,1)} %dynamic-slice_bitcast_fusion.4), channel_id=1, source_target_pairs={{0,1},{1,0},{2,3},{3,2},{4,5},{5,4},{6,7},{7,6},{8,9},{9,8},{10,11... | collective-permute-start | bytes 6291464 | tf_op jit(solution)/shard_map/ppermute | solution.py:257
  256.3 9.4 %copy-start.18 = (bf16[8,256,1024]{2,1,0:T(8,128)(2,1)S(1)}, bf16[8,256,1024]{2,1,0:T(8,128)(2,1)}, u32[]{:S(2)}) copy-start(bf16[8,256,1024]{2,1,0:T(8,128)(2,1)} %copy-done.17) | copy-start | bytes 12582916
  274.2 41.8 %collective-permute-start.3 = (bf16[8,64,4096]{2,1,0:T(8,128)(2,1)}, bf16[8,64,4096]{2,1,0:T(8,128)(2,1)}, u32[]{:S(2)}, u32[]{:S(2)}) collective-permute-start(bf16[8,64,4096]{2,1,0:T(8,128)(2,1)} %dynamic-slice_bitcast_fusion.1), channel_id=1, source_target_pairs={{0,2},{2,0},{4,6},{6,4},{8,10},{10,8},{12,14},{14,12},{16,18},{18,... | collective-permute-start | bytes 12582920 | tf_op jit(solution)/shard_map/ppermute | solution.py:257
  274.5 181.2 %reduce-scatter.6.cloned.1.call-start = ((), (), s32[]{:S(2)}) async-start(), calls=%async_computation.7 | async-start | bytes 4718592 | tf_op jit(solution)/shard_map/reduce_scatter | solution.py:277
  283.5 1.2 copy-start.27
  284.2 4.2 copy-start.14
  285.3 3.1 copy-start.8
  285.3 3.1 copy-start.11
  288.4 20.6 %copy-start.5 = (bf16[512,1024]{1,0:T(8,128)(2,1)}, bf16[512,1024]{1,0:T(8,128)(2,1)S(1)}, u32[]{:S(2)}) copy-start(bf16[512,1024]{1,0:T(8,128)(2,1)S(1)} %fusion.40.g_ref) | copy-start | bytes 3145732
  309.0 1.3 copy-start.13
  310.4 32.9 %collective-permute-start.4 = (bf16[512,1024]{1,0:T(8,128)(2,1)}, bf16[512,1024]{1,0:T(8,128)(2,1)}, u32[]{:S(2)}, u32[]{:S(2)}) collective-permute-start(bf16[512,1024]{1,0:T(8,128)(2,1)} %get-tuple-element.51), channel_id=1, source_target_pairs={{1,0},{3,2},{5,4},{7,6},{9,8},{11,10},{13,12},{15,14},{17,16},{19,... | collective-permute-start | bytes 3145736 | tf_op jit(solution)/shard_map/ppermute | solution.py:388
  311.7 48.7 %collective-permute-start.5 = (bf16[512,1024]{1,0:T(8,128)(2,1)}, bf16[512,1024]{1,0:T(8,128)(2,1)}, u32[]{:S(2)}, u32[]{:S(2)}) collective-permute-start(bf16[512,1024]{1,0:T(8,128)(2,1)} %get-tuple-element.53), channel_id=1, source_target_pairs={{1,0},{3,2},{5,4},{7,6},{9,8},{11,10},{13,12},{15,14},{17,16},{19,... | collective-permute-start | bytes 3145736 | tf_op jit(solution)/shard_map/ppermute | solution.py:389
  316.0 7.4 %copy-start.2 = (bf16[512,2048]{1,0:T(8,128)(2,1)S(1)}, bf16[512,2048]{1,0:T(8,128)(2,1)}, u32[]{:S(2)}) copy-start(bf16[512,2048]{1,0:T(8,128)(2,1)} %copy-done.1) | copy-start | bytes 6291460
  316.0 7.4 %copy-start.4 = (bf16[512,1024]{1,0:T(8,128)(2,1)S(1)}, bf16[512,1024]{1,0:T(8,128)(2,1)}, u32[]{:S(2)}) copy-start(bf16[512,1024]{1,0:T(8,128)(2,1)} %copy-done.3) | copy-start | bytes 3145732
  316.0 7.4 %copy-start.6 = (bf16[512,1024]{1,0:T(8,128)(2,1)S(1)}, bf16[512,1024]{1,0:T(8,128)(2,1)}, u32[]{:S(2)}) copy-start(bf16[512,1024]{1,0:T(8,128)(2,1)} %copy-done.5) | copy-start | bytes 3145732
  316.0 7.4 %copy-start.9 = (bf16[512,1024]{1,0:T(8,128)(2,1)S(1)}, bf16[512,1024]{1,0:T(8,128)(2,1)}, u32[]{:S(2)}) copy-start(bf16[512,1024]{1,0:T(8,128)(2,1)} %copy-done.7) | copy-start | bytes 3145732
  316.0 7.4 %copy-start.12 = (f32[512,1024]{1,0:T(8,128)S(1)}, f32[512,1024]{1,0:T(8,128)}, u32[]{:S(2)}) copy-start(f32[512,1024]{1,0:T(8,128)} %copy-done.10) | copy-start | bytes 6291460
  342.0 1.3 copy-start
  343.3 18.6 %copy-start.21 = (bf16[1,512,1024]{2,1,0:T(8,128)(2,1)S(1)}, bf16[1,512,1024]{2,1,0:T(8,128)(2,1)}, u32[]{:S(2)}) copy-start(bf16[1,512,1024]{2,1,0:T(8,128)(2,1)} %param.14) | copy-start | bytes 3145732
  345.6 24.6 %copy-start.29 = (bf16[512,1024]{1,0:T(8,128)(2,1)}, bf16[512,1024]{1,0:T(8,128)(2,1)S(1)}, u32[]{:S(2)}) copy-start(bf16[512,1024]{1,0:T(8,128)(2,1)S(1)} %add_convert_fusion.2) | copy-start | bytes 3145732
  361.9 8.3 %copy-start.31 = (bf16[512,1024]{1,0:T(8,128)(2,1)}, bf16[512,1024]{1,0:T(8,128)(2,1)S(1)}, u32[]{:S(2)}) copy-start(bf16[512,1024]{1,0:T(8,128)(2,1)S(1)} %add_convert_fusion.1) | copy-start | bytes 3145732
  370.2 1.2 copy-start.22
  370.2 3.8 copy-start.30
  370.3 206.8 %reduce-scatter.8.cloned.1.call-start = ((), (), s32[]{:S(2)}) async-start(), calls=%async_computation.8 | async-start | bytes 2433024 | tf_op jit(solution)/shard_map/reduce_scatter | solution.py:277
  370.3 3.7 copy-start.32
  375.2 5.1 copy-start.33
  381.5 7.4 %collective-permute-start.6 = (bf16[8,64,4224]{2,1,0:T(8,128)(2,1)S(1)}, bf16[8,64,4224]{2,1,0:T(8,128)(2,1)S(1)}, u32[]{:S(2)}, u32[]{:S(2)}) collective-permute-start(bf16[8,64,4224]{2,1,0:T(8,128)(2,1)S(1)} %dynamic-slice_bitcast_fusion), channel_id=1, source_target_pairs={{0,2},{2,0},{4,6},{6,4},{8,10},{10,8},{12,14},{14,12},{16,18},{18,... | collective-permute-start | bytes 12976136 | tf_op jit(solution)/shard_map/ppermute | solution.py:257
  455.7 50.8 %copy-start.16 = (bf16[8,64,4224]{2,1,0:T(8,128)(2,1)S(1)}, bf16[8,64,4224]{2,1,0:T(8,128)(2,1)}, u32[]{:S(2)}) copy-start(bf16[8,64,4224]{2,1,0:T(8,128)(2,1)} %fusion) | copy-start | bytes 12976132
  457.6 50.8 %copy-start.36 = (f32[16,64]{1,0:T(8,128)S(1)}, f32[16,64]{1,0:T(8,128)}, u32[]{:S(2)}) copy-start(f32[16,64]{1,0:T(8,128)} %get-tuple-element.76) | copy-start | bytes 12292
  457.6 48.9 %collective-permute-start.7 = (bf16[8,32,4224]{2,1,0:T(8,128)(2,1)S(1)}, bf16[8,32,4224]{2,1,0:T(8,128)(2,1)S(1)}, u32[]{:S(2)}, u32[]{:S(2)}) collective-permute-start(bf16[8,32,4224]{2,1,0:T(8,128)(2,1)S(1)} %dynamic-slice_bitcast_fusion.3), channel_id=1, source_target_pairs={{0,1},{1,0},{2,3},{3,2},{4,5},{5,4},{6,7},{7,6},{8,9},{9,8},{10,11... | collective-permute-start | bytes 6488072 | tf_op jit(solution)/shard_map/ppermute | solution.py:257
  508.5 11.2 %copy-start.35 = (bf16[128,1024]{1,0:T(8,128)(2,1)S(1)}, bf16[128,1024]{1,0:T(8,128)(2,1)}, u32[]{:S(2)}) copy-start(bf16[128,1024]{1,0:T(8,128)(2,1)} %reduce-scatter.4.cloned.1.call-done) | copy-start | bytes 786436
  508.5 12.7 %copy-start.34 = (bf16[64,4096]{1,0:T(8,128)(2,1)S(1)}, bf16[64,4096]{1,0:T(8,128)(2,1)}, u32[]{:S(2)}) copy-start(bf16[64,4096]{1,0:T(8,128)(2,1)} %reduce-scatter.6.cloned.1.call-done) | copy-start | bytes 1572868
  508.5 13.2 %copy-start.15 = (f32[512,1024]{1,0:T(8,128)S(1)}, f32[512,1024]{1,0:T(8,128)}, u32[]{:S(2)}) copy-start(f32[512,1024]{1,0:T(8,128)} %copy-done.14) | copy-start | bytes 6291460
  508.5 13.2 %copy-start.23 = (f32[512,1024]{1,0:T(8,128)S(1)}, f32[512,1024]{1,0:T(8,128)}, u32[]{:S(2)}) copy-start(f32[512,1024]{1,0:T(8,128)} %get-tuple-element.93) | copy-start | bytes 6291460
  508.5 13.2 %copy-start.28 = (bf16[1,512,1024]{2,1,0:T(8,128)(2,1)S(1)}, bf16[1,512,1024]{2,1,0:T(8,128)(2,1)}, u32[]{:S(2)}) copy-start(bf16[1,512,1024]{2,1,0:T(8,128)(2,1)} %param.15) | copy-start | bytes 3145732
  519.7 9.2 %collective-permute-start.10 = (bf16[128,1024]{1,0:T(8,128)(2,1)S(1)}, bf16[128,1024]{1,0:T(8,128)(2,1)S(1)}, u32[]{:S(2)}, u32[]{:S(2)}) collective-permute-start(bf16[128,1024]{1,0:T(8,128)(2,1)S(1)} %copy-done.35), channel_id=1, source_target_pairs={{0,1},{1,0},{2,3},{3,2},{4,5},{5,4},{6,7},{7,6},{8,9},{9,8},{10,11... | collective-permute-start | bytes 786440 | tf_op jit(solution)/shard_map/ppermute | solution.py:289
  521.3 57.4 %collective-permute-start.9 = (bf16[64,4096]{1,0:T(8,128)(2,1)S(1)}, bf16[64,4096]{1,0:T(8,128)(2,1)S(1)}, u32[]{:S(2)}, u32[]{:S(2)}) collective-permute-start(bf16[64,4096]{1,0:T(8,128)(2,1)S(1)} %copy-done.34), channel_id=1, source_target_pairs={{0,1},{1,0},{2,3},{3,2},{4,5},{5,4},{6,7},{7,6},{8,9},{9,8},{10,11... | collective-permute-start | bytes 1572872 | tf_op jit(solution)/shard_map/ppermute | solution.py:289
  577.0 7.5 %collective-permute-start.8 = (bf16[32,4224]{1,0:T(8,128)(2,1)}, bf16[32,4224]{1,0:T(8,128)(2,1)S(1)}, u32[]{:S(2)}, u32[]{:S(2)}) collective-permute-start(bf16[32,4224]{1,0:T(8,128)(2,1)} %reduce-scatter.8.cloned.1.call-done), channel_id=1, source_target_pairs={{0,1},{1,0},{2,3},{3,2},{4,5},{5,4},{6,7},{7,6},{8,9},{9,8},{10,11... | collective-permute-start | bytes 811016 | tf_op jit(solution)/shard_map/ppermute | solution.py:289
Sparse Core Ops, SparseCore 0:
  11.6 79.2 all-gather.3
  93.0 73.0 all-gather.5
  168.3 73.1 all-gather.7
  274.6 66.0 reduce-scatter.3
  370.4 85.2 reduce-scatter.5
  508.6 68.4 reduce-scatter.7
